TPU v7x, 128 devices: a whole 4x4x4 slice. The times are simulated.
128 devices in a mesh: ta: 16 (over y_hi, x, core), gz: 8 (over z, y_lo).
Axes of the slice: x: 4, y: 4 (y_hi: 2, y_lo: 2; y = y_hi * 2 + y_lo), z: 4, core: 2. Of those that a mesh axis runs over, the one named last changes fastest.
Arguments:
- gauge_links: float32 [4, 2, 3, 3, 16, 64, 1024], P(None, None, None, None, 'ta', 'gz'), may hold values from -1 to 1, as said below
Outputs:
- rotated: float32 [4, 2, 3, 3, 16, 64, 1024], P(None, None, None, None, 'ta', 'gz')
Inputs may be any that keep to these rules, and one draw needn't show every extreme that they name: `gauge_links`: every link is a special unitary 3x3 matrix.
All inputs are finite; a program needn't handle non-finite values.
Results may differ from a plain program's by a relative error of at most 0.0001.
Values sent between devices are 32-bit elements; how exact they have to be, the bound alone decides.
A program may use at most 192 MiB of HBM per device.

v0:
```python
import jax
import jax.numpy as jnp
from jax import lax
from jax.sharding import PartitionSpec as P

LX = 32
LY = 32
ITERS = 2


def passed_along(block, axis, distance):
    devices = range(lax.axis_size(axis))
    route = [((i - distance) % len(devices), i) for i in devices]
    return lax.ppermute(block, axis, route)


def with_halo(block, sides, width):
    for axis, dim in sides:
        count = lax.axis_size(axis)
        forward = [(i, i + 1) for i in range(count - 1)]
        forward.append((count - 1, 0))
        backward = [(target, source) for source, target in forward]
        low = lax.ppermute(
            lax.slice_in_dim(block, block.shape[dim] - width, None, axis=dim), axis, forward
        )
        high = lax.ppermute(lax.slice_in_dim(block, 0, width, axis=dim), axis, backward)
        block = jnp.concatenate([low, block, high], axis=dim)
    return block


def matrix_product(left_real, left_imag, right_real, right_imag):
    out_real = []
    out_imag = []
    for row_index in range(3):
        real_row = []
        imag_row = []
        for column in range(3):
            total_real = (
                left_real[row_index, 0] * right_real[0, column]
                - left_imag[row_index, 0] * right_imag[0, column]
            )
            total_imag = (
                left_real[row_index, 0] * right_imag[0, column]
                + left_imag[row_index, 0] * right_real[0, column]
            )
            for inner_index in (1, 2):
                total_real = (
                    total_real
                    + left_real[row_index, inner_index] * right_real[inner_index, column]
                    - left_imag[row_index, inner_index] * right_imag[inner_index, column]
                )
                total_imag = (
                    total_imag
                    + left_real[row_index, inner_index] * right_imag[inner_index, column]
                    + left_imag[row_index, inner_index] * right_real[inner_index, column]
                )
            real_row.append(total_real)
            imag_row.append(total_imag)
        out_real.append(jnp.stack(real_row))
        out_imag.append(jnp.stack(imag_row))
    return (jnp.stack(out_real), jnp.stack(out_imag))


def adjoint(matrix_real, matrix_imag):
    return (jnp.swapaxes(matrix_real, 0, 1), -jnp.swapaxes(matrix_imag, 0, 1))


def identity_like(matrix_real):
    return jnp.eye(3, dtype=jnp.float32).reshape((3, 3) + (1,) * (matrix_real.ndim - 2))


def antihermitian(w_real, w_imag):
    part_real = 0.5 * (w_real - jnp.swapaxes(w_real, 0, 1))
    part_imag = 0.5 * (w_imag + jnp.swapaxes(w_imag, 0, 1))
    trace_third = (w_imag[0, 0] + w_imag[1, 1] + w_imag[2, 2]) / 3.0
    return (part_real, part_imag - identity_like(w_real) * trace_third[None, None])


def normalized(row_real, row_imag):
    factor = 1.0 / jnp.sqrt(jnp.sum(row_real * row_real + row_imag * row_imag, axis=0))
    return (row_real * factor, row_imag * factor)


def conjugate_cross(first_real, first_imag, second_real, second_imag):
    third_real = []
    third_imag = []
    for position in range(3):
        follow = (position + 1) % 3
        beyond = (position + 2) % 3
        cross_real = (
            first_real[follow] * second_real[beyond]
            - first_imag[follow] * second_imag[beyond]
            - (first_real[beyond] * second_real[follow] - first_imag[beyond] * second_imag[follow])
        )
        cross_imag = (
            first_real[follow] * second_imag[beyond]
            + first_imag[follow] * second_real[beyond]
            - (first_real[beyond] * second_imag[follow] + first_imag[beyond] * second_real[follow])
        )
        third_real.append(cross_real)
        third_imag.append(-cross_imag)
    return (jnp.stack(third_real), jnp.stack(third_imag))


def unitary_projection(power_real, power_imag):
    first_real, first_imag = normalized(power_real[0], power_imag[0])
    proj_real = jnp.sum(first_real * power_real[1] + first_imag * power_imag[1], axis=0)
    proj_imag = jnp.sum(first_real * power_imag[1] - first_imag * power_real[1], axis=0)
    second_real = power_real[1] - (proj_real * first_real - proj_imag * first_imag)
    second_imag = power_imag[1] - (proj_real * first_imag + proj_imag * first_real)
    second_real, second_imag = normalized(second_real, second_imag)
    third_real, third_imag = conjugate_cross(first_real, first_imag, second_real, second_imag)
    gauge_real = jnp.stack([first_real, second_real, third_real])
    gauge_imag = jnp.stack([first_imag, second_imag, third_imag])
    return (gauge_real, gauge_imag)


def second_order_exponential(smooth_real, smooth_imag):
    exponent_real = 0.04 * smooth_real
    exponent_imag = 0.04 * smooth_imag
    square_real, square_imag = matrix_product(
        exponent_real, exponent_imag, exponent_real, exponent_imag
    )
    power_real = identity_like(smooth_real) + exponent_real + 0.5 * square_real
    power_imag = exponent_imag + 0.5 * square_imag
    return unitary_projection(power_real, power_imag)


def rotate_link(left_side, link_now, right_side):
    product_real, product_imag = matrix_product(
        left_side[0], left_side[1], link_now[0], link_now[1]
    )
    adjoint_real, adjoint_imag = adjoint(right_side[0], right_side[1])
    new_real, new_imag = matrix_product(product_real, product_imag, adjoint_real, adjoint_imag)
    return jnp.stack([new_real, new_imag])


def displace(array, direction, amount):
    if direction == 1:
        return jnp.roll(array, amount * LX, axis=-1)
    sites = array.shape[-1]
    column_x = jnp.arange(sites, dtype=jnp.int32) % LX
    edge = 0 if amount == 1 else LX - 1
    inside = jnp.roll(array, amount, axis=-1)
    wrapped = jnp.roll(array, amount - amount * LX, axis=-1)
    return jnp.where(column_x == edge, wrapped, inside)


def lattice_sine(mode_index, length):
    sine_value = jnp.sin(jnp.pi * mode_index.astype(jnp.float32) / length)
    return 4.0 * sine_value * sine_value


def dense_table(first_length, second_length):
    count = first_length * second_length
    index = jnp.arange(count, dtype=jnp.int32)
    inner = index % first_length
    outer = index // first_length
    phase_inner = inner[:, None] * inner[None, :] % first_length
    phase_outer = outer[:, None] * outer[None, :] % second_length
    angles = (
        2.0
        * jnp.pi
        * (
            phase_inner.astype(jnp.float32) / first_length
            + phase_outer.astype(jnp.float32) / second_length
        )
    )
    cosine = jnp.cos(angles)
    sine_value = jnp.sin(angles)
    return jnp.concatenate(
        [
            jnp.concatenate([cosine, -sine_value], axis=1),
            jnp.concatenate([sine_value, cosine], axis=1),
        ],
        axis=0,
    )


def forward_apply(rows, table):
    return jnp.dot(rows, table, precision=lax.Precision.HIGHEST, preferred_element_type=jnp.float32)


def backward_apply(rows, table, factor):
    return (
        jnp.einsum(
            "rq,pq->rp",
            rows,
            table,
            precision=lax.Precision.HIGHEST,
            preferred_element_type=jnp.float32,
        )
        * factor
    )


def spectral_weight(time_length, depth_length, columns):
    plane_sites = LX * LY
    offset = lax.axis_index("ta") * (plane_sites // lax.axis_size("ta")) + lax.axis_index("gz") * (
        plane_sites // (lax.axis_size("ta") * lax.axis_size("gz"))
    )
    column_index = offset + jnp.arange(columns, dtype=jnp.int32)
    wave_y = column_index // LX
    wave_x = column_index % LX
    line_index = jnp.arange(time_length * depth_length, dtype=jnp.int32)
    time_modes = line_index // depth_length
    depth_modes = line_index % depth_length
    summed = (lattice_sine(wave_y, LY) + lattice_sine(wave_x, LX))[:, None] + (
        lattice_sine(time_modes, time_length) + lattice_sine(depth_modes, depth_length)
    )[None, :]
    anchor = (column_index[:, None] == 0) & (line_index[None, :] == 0)
    return jnp.where(anchor, 0.0, 16.0 / jnp.where(anchor, 1.0, summed))


def smooth_field(delta_real, delta_imag, plane_table, line_table):
    real_side = delta_real.reshape((9,) + delta_real.shape[2:])
    imag_side = delta_imag.reshape((9,) + delta_imag.shape[2:])
    stacked = jnp.stack([real_side, imag_side], axis=3)
    layout = stacked.shape
    count, local_time, local_depth, pair, sites = layout
    plane = forward_apply(
        stacked.reshape(count * local_time * local_depth, 2 * sites), plane_table
    ).reshape(layout)
    spectral = lax.all_to_all(
        lax.all_to_all(plane, "ta", split_axis=4, concat_axis=1, tiled=True),
        "gz",
        split_axis=4,
        concat_axis=2,
        tiled=True,
    )
    time_length = spectral.shape[1]
    depth_length = spectral.shape[2]
    columns = spectral.shape[4]
    lines = time_length * depth_length
    ordered = jnp.transpose(spectral, (0, 4, 3, 1, 2)).reshape(count * columns, 2 * lines)
    ordered = forward_apply(ordered, line_table).reshape(count, columns, 2, lines)
    ordered = ordered * spectral_weight(time_length, depth_length, columns)[None, :, None, :]
    ordered = backward_apply(ordered.reshape(count * columns, 2 * lines), line_table, 1.0 / lines)
    ordered = ordered.reshape(count, columns, 2, time_length, depth_length)
    spectral = jnp.transpose(ordered, (0, 3, 4, 2, 1)).reshape(
        count, time_length, depth_length, 2, 1, columns
    )
    spectral = lax.all_to_all(
        lax.all_to_all(spectral, "ta", split_axis=1, concat_axis=4, tiled=True),
        "gz",
        split_axis=2,
        concat_axis=5,
        tiled=True,
    )
    plane = spectral.reshape(count * local_time * local_depth, 2 * sites)
    smooth = backward_apply(plane, plane_table, 1.0 / sites).reshape(layout)
    real_part = smooth[:, :, :, 0]
    imag_part = smooth[:, :, :, 1]
    smooth_real = real_part.reshape((3, 3) + real_part.shape[1:])
    smooth_imag = imag_part.reshape((3, 3) + imag_part.shape[1:])
    return (smooth_real, smooth_imag)


def on_device(gauge_links):
    lattice = gauge_links
    local_time = lattice.shape[4]
    local_depth = lattice.shape[5]
    plane_table = dense_table(LX, LY)
    line_table = dense_table(local_depth * lax.axis_size("gz"), local_time * lax.axis_size("ta"))
    lower_time = passed_along(lattice[3, :, :, :, local_time - 1], "ta", 1)
    lower_depth = passed_along(lattice[2, :, :, :, :, local_depth - 1], "gz", 1)
    for iteration in range(ITERS):
        summed = jnp.zeros(lattice.shape[1:], jnp.float32)
        for direction in range(4):
            link_now = lattice[direction]
            if direction == 3:
                behind = jnp.concatenate(
                    [lower_time[:, :, :, None], link_now[:, :, :, :-1]], axis=3
                )
            elif direction == 2:
                behind = jnp.concatenate(
                    [lower_depth[:, :, :, :, None], link_now[:, :, :, :, :-1]], axis=4
                )
            else:
                behind = displace(link_now, direction, 1)
            summed = summed + behind - link_now
        delta_real, delta_imag = antihermitian(summed[0], summed[1])
        smooth_real, smooth_imag = smooth_field(delta_real, delta_imag, plane_table, line_table)
        gauge_real, gauge_imag = second_order_exponential(smooth_real, smooth_imag)
        gauge = jnp.stack([gauge_real, gauge_imag])
        padded = with_halo(gauge, (("ta", 3), ("gz", 4)), 1)
        rotated = []
        for direction in range(4):
            if direction == 3:
                forward = padded[:, :, :, 2:, 1:-1]
            elif direction == 2:
                forward = padded[:, :, :, 1:-1, 2:]
            else:
                forward = displace(gauge, direction, -1)
            rotated.append(rotate_link(gauge, lattice[direction], forward))
        if iteration + 1 < ITERS:
            lower_time = rotate_link(padded[:, :, :, 0, 1:-1], lower_time, gauge[:, :, :, 0])
            lower_depth = rotate_link(padded[:, :, :, 1:-1, 0], lower_depth, gauge[:, :, :, :, 0])
        lattice = jnp.stack(rotated)
    return lattice


def solution(mesh):
    in_specs = (P(None, None, None, None, "ta", "gz", None),)
    out_specs = P(None, None, None, None, "ta", "gz", None)
    return jax.shard_map(
        on_device, mesh=mesh, in_specs=in_specs, out_specs=out_specs, check_vma=False
    )
```

profile of v0, /device:TPU:1, one launch (start us, length us, event | category | flops | bytes accessed | tf_op | source)
XLA Modules:
  0.0 686.1 jit_solution(5923757541020745693)
XLA Ops:
  16.0 24.2 %fusion.18 = (f32[1024,1024]{0,1:T(8,128)}, f32[1024,1024]{0,1:T(8,128)}, f32[1024,1024]{0,1:T(8,128)}) fusion(s32[1024]{0:T(1024)S(1)} %get-tuple-element.179, s32[1024]{0:T(1024)} %get-tuple-element.180), kind=kLoop, calls=%fused_computation.47 | loop fusion | flops 30408704 | bytes 12591104 | tf_op jit(solution)/shard_map/neg | solution.py:173
  40.2 23.1 %fusion.19 = (f32[1024,1024]{0,1:T(8,128)}, f32[1024,1024]{0,1:T(8,128)}, f32[1024,1024]{0,1:T(8,128)}) fusion(s32[1024]{0:T(1024)S(1)} %get-tuple-element.175, s32[1024]{0:T(1024)S(1)} %get-tuple-element.176), kind=kLoop, calls=%fused_computation.48 | loop fusion | flops 32505856 | bytes 12591104 | tf_op jit(solution)/shard_map/neg | solution.py:173
  63.4 10.3 %maximum_maximum_fusion = f32[2048,2048]{0,1:T(8,128)S(1)} fusion(f32[1024,1024]{0,1:T(8,128)} %get-tuple-element.171, f32[1024,1024]{0,1:T(8,128)} %get-tuple-element.170, f32[1024,1024]{0,1:T(8,128)} %get-tuple-element.169), kind=kLoop, calls=%fused_computation | loop fusion | flops 12582912 | bytes 29360128 | tf_op jit(solution)/shard_map/concatenate | solution.py:171
  79.7 16.6 %convolution_bitcast_fusion.1 = f32[9,1,8,2,1024]{4,2,3,0,1:T(8,128)S(1)} fusion(f32[9,8,2048,1]{2,1,3,0:T(8,128)S(1)} %bitcast.5507, f32[2,1024,2048,1]{2,1,0,3:T(8,128)S(1)} %bitcast.5414), kind=kOutput, calls=%fused_computation.76 | convolution fusion | flops 3623878656 | bytes 17956864 | tf_op jit(solution)/shard_map/dot_general | solution.py:181
  102.6 8.6 %reshape.64562 = f32[16,1,9216]{2,1,0:T(1,128)} reshape(f32[1024,1,2,8,9]{4,3,2,1,0:T(8,128)} %bitcast.5395) | data formatting | bytes 1179648
  117.7 15.6 %maximum_maximum_fusion.1 = f32[2048,2048]{0,1:T(8,128)} fusion(f32[1024,1024]{0,1:T(8,128)} %get-tuple-element.174, f32[1024,1024]{0,1:T(8,128)} %get-tuple-element.173, f32[1024,1024]{0,1:T(8,128)} %get-tuple-element.172), kind=kLoop, calls=%fused_computation.1 | loop fusion | flops 12582912 | bytes 29360128 | tf_op jit(solution)/shard_map/concatenate | solution.py:171
  135.8 10.9 %reshape.64563 = f32[1024,1,2,8,9]{4,3,2,1,0:T(8,128)} reshape(f32[16,9216]{1,0:T(8,128)S(1)} %reduce.8) | data formatting | bytes 1179648
  146.6 11.8 %copy.2299 = f32[9,1,8,2,16,64]{4,3,2,0,5,1:T(2,128)} copy(f32[9,1,8,2,16,64]{0,2,3,5,4,1:T(8,128)} %bitcast.5396) | data formatting | bytes 1179648 | tf_op jit(solution)/shard_map/all_to_all | solution.py:225
  164.6 8.8 %reshape.64564 = f32[8,1,18432]{2,1,0:T(1,128)} reshape(f32[64,9,8,2,16]{4,3,2,1,0:T(2,128)} %bitcast_bitcast_fusion.1) | data formatting | bytes 1179648
  179.7 9.5 %all-to-all-done.1 = f32[8,1,18432]{2,1,0:T(1,128)S(1)} async-done(((f32[8,1,18432]{2,1,0:T(1,128)}), f32[8,1,18432]{2,1,0:T(1,128)S(1)}, u32[]{:S(2)}, u32[]{:S(2)}) %all-to-all-start.1) | async-done | bytes 589856 | tf_op jit(solution)/shard_map/all_to_all | solution.py:224
  191.2 8.4 %reshape.64565 = f32[64,9,8,2,16]{4,3,2,1,0:T(2,128)} reshape(f32[8,18432]{1,0:T(8,128)S(1)} %reduce.9) | data formatting | bytes 1179648
  210.5 20.0 %convolution_multiply_fusion.5 = f32[9,8,2,1024]{3,1,2,0:T(8,128)S(1)} fusion(f32[2,1024,2048,1]{2,1,0,3:T(8,128)} %bitcast.5418, f32[9,8,2048,1]{2,1,0,3:T(8,128)} %reshape.64556, f32[8,1024]{1,0:T(8,128)} %and_select_fusion), kind=kOutput, calls=%fused_computation.78 | convolution fusion | flops 3624026112 | bytes 17989632 | tf_op jit(solution)/shard_map/dot_general | solution.py:181
  230.5 18.3 %convolution_multiply_fusion.3 = f32[72,2048]{1,0:T(8,128)} fusion(f32[72,2048]{1,0:T(8,128)S(1)} %bitcast.5510, f32[1024,1024]{0,1:T(8,128)} %get-tuple-element.174, f32[1024,1024]{0,1:T(8,128)} %get-tuple-element.173, f32[1024,1024]{0,1:T(8,128)} %get-tuple-element.172), kind=kOutput, calls=%fused_computation.42 | convolution fusion | flops 3636609024 | bytes 13762560 | tf_op jit(solution)/shard_map/rq,pq->rp/dot_general | solution.py:186
  254.8 9.2 %all-to-all-start.2 = ((f32[16,1,9216]{2,1,0:T(1,128)}), f32[16,1,9216]{2,1,0:T(1,128)}, u32[]{:S(2)}, u32[]{:S(2)}) async-start(f32[16,1,9216]{2,1,0:T(1,128)} %reshape.64566), calls=%async_computation.2 | async-start | bytes 1179648 | tf_op jit(solution)/shard_map/all_to_all | solution.py:244
  265.3 11.0 %all-to-all-done.2 = f32[16,1,9216]{2,1,0:T(1,128)} async-done(((f32[16,1,9216]{2,1,0:T(1,128)}), f32[16,1,9216]{2,1,0:T(1,128)}, u32[]{:S(2)}, u32[]{:S(2)}) %all-to-all-start.2) | async-done | bytes 589856 | tf_op jit(solution)/shard_map/all_to_all | solution.py:244
  292.5 8.3 %all-to-all-done.3 = f32[8,1,18432]{2,1,0:T(1,128)S(1)} async-done(((f32[8,1,18432]{2,1,0:T(1,128)}), f32[8,1,18432]{2,1,0:T(1,128)S(1)}, u32[]{:S(2)}, u32[]{:S(2)}) %all-to-all-start.3) | async-done | bytes 589856 | tf_op jit(solution)/shard_map/all_to_all | solution.py:243
  311.6 7.7 %copy.2306 = f32[9,1,8,2,16,8,8]{6,5,4,3,2,0,1:T(8,128)} copy(f32[9,1,8,2,16,8,8]{4,6,3,2,5,0,1:T(8,128)} %bitcast.5402) | data formatting | bytes 1179648 | tf_op jit(solution)/shard_map/all_to_all | solution.py:243
  326.7 17.5 %convolution_multiply_fusion.2 = f32[72,2048]{1,0:T(8,128)S(1)} fusion(f32[72,2048]{1,0:T(8,128)S(1)} %reshape.63778, f32[1024,1024]{0,1:T(8,128)} %get-tuple-element.171, f32[1024,1024]{0,1:T(8,128)} %get-tuple-element.170, f32[1024,1024]{0,1:T(8,128)} %get-tuple-element.169), kind=kOutput, calls=%fused_computation.41 | convolution fusion | flops 3636609024 | bytes 13762560 | tf_op jit(solution)/shard_map/rq,pq->rp/dot_general | solution.py:186
  375.0 17.2 %convolution_bitcast_fusion = f32[9,1,8,2,1024]{4,2,3,0,1:T(8,128)} fusion(f32[9,8,2048,1]{2,1,3,0:T(8,128)S(1)} %bitcast.5506, f32[2,1024,2048,1]{2,1,0,3:T(8,128)S(1)} %bitcast.5417), kind=kOutput, calls=%fused_computation.75 | convolution fusion | flops 3623878656 | bytes 17956864 | tf_op jit(solution)/shard_map/dot_general | solution.py:181
  399.3 8.6 %reshape.64570 = f32[16,1,9216]{2,1,0:T(1,128)} reshape(f32[1024,1,2,8,9]{4,3,2,1,0:T(8,128)} %bitcast.5397) | data formatting | bytes 1179648
  408.0 22.7 %all_to_all.138 = f32[16,1,9216]{2,1,0:T(1,128)} all-to-all(f32[16,1,9216]{2,1,0:T(1,128)} %reshape.64570), channel_id=1, replica_groups=mesh['ta'=16,'gz'=8] {'ta'}, dimensions={0} | all-to-all | bytes 1179648 | tf_op jit(solution)/shard_map/all_to_all | solution.py:225
  434.5 11.8 %reshape.64571 = f32[1024,1,2,8,9]{4,3,2,1,0:T(8,128)} reshape(f32[16,9216]{1,0:T(8,128)} %reduce.12) | data formatting | bytes 1179648
  446.4 11.8 %copy.2621 = f32[9,1,8,2,16,64]{4,3,2,0,5,1:T(2,128)} copy(f32[9,1,8,2,16,64]{0,2,3,5,4,1:T(8,128)} %bitcast.5398) | data formatting | bytes 1179648 | tf_op jit(solution)/shard_map/all_to_all | solution.py:225
  464.3 8.7 %reshape.64572 = f32[8,1,18432]{2,1,0:T(1,128)} reshape(f32[64,9,8,2,16]{4,3,2,1,0:T(2,128)} %bitcast_bitcast_fusion) | data formatting | bytes 1179648
  473.0 14.9 %all_to_all.139 = f32[8,1,18432]{2,1,0:T(1,128)} all-to-all(f32[8,1,18432]{2,1,0:T(1,128)} %reshape.64572), channel_id=1, replica_groups=mesh['ta'=16,'gz'=8] {'gz'}, dimensions={0} | all-to-all | bytes 1179648 | tf_op jit(solution)/shard_map/all_to_all | solution.py:224
  491.8 9.6 %reshape.64573 = f32[64,9,8,2,16]{4,3,2,1,0:T(2,128)} reshape(f32[8,18432]{1,0:T(8,128)} %reduce.13) | data formatting | bytes 1179648
  514.4 20.4 %convolution_multiply_fusion.4 = f32[9,8,2,1024]{3,1,2,0:T(8,128)} fusion(f32[2,1024,2048,1]{2,1,0,3:T(8,128)} %bitcast.5419, f32[9,8,2048,1]{2,1,0,3:T(8,128)} %reshape.64559, f32[8,1024]{1,0:T(8,128)S(1)} %copy-done.15), kind=kOutput, calls=%fused_computation.77 | convolution fusion | flops 3624026112 | bytes 17989632 | tf_op jit(solution)/shard_map/dot_general | solution.py:181
  534.8 18.3 %convolution_multiply_fusion.1 = f32[72,2048]{1,0:T(8,128)} fusion(f32[72,2048]{1,0:T(8,128)} %bitcast.5509, f32[1024,1024]{0,1:T(8,128)} %get-tuple-element.174, f32[1024,1024]{0,1:T(8,128)} %get-tuple-element.173, f32[1024,1024]{0,1:T(8,128)} %get-tuple-element.172), kind=kOutput, calls=%fused_computation.40 | convolution fusion | flops 3636609024 | bytes 13762560 | tf_op jit(solution)/shard_map/rq,pq->rp/dot_general | solution.py:186
  561.4 18.6 %all_to_all.140 = f32[16,1,9216]{2,1,0:T(1,128)} all-to-all(f32[16,1,9216]{2,1,0:T(1,128)} %reshape.64574), channel_id=1, replica_groups=mesh['ta'=16,'gz'=8] {'ta'}, dimensions={0} | all-to-all | bytes 1179648 | tf_op jit(solution)/shard_map/all_to_all | solution.py:244
  597.2 14.5 %all_to_all.141 = f32[8,1,18432]{2,1,0:T(1,128)} all-to-all(f32[8,1,18432]{2,1,0:T(1,128)} %reshape.64576), channel_id=1, replica_groups=mesh['ta'=16,'gz'=8] {'gz'}, dimensions={0} | all-to-all | bytes 1179648 | tf_op jit(solution)/shard_map/all_to_all | solution.py:243
  633.1 8.1 %reshape.63784 = f32[72,2048]{1,0:T(8,128)} reshape(f32[9,1,8,2,16,8,8]{6,5,4,3,2,0,1:T(8,128)} %copy.2628) | data formatting | bytes 1179648 | tf_op jit(solution)/shard_map/reshape | solution.py:250
  641.2 18.5 %convolution_multiply_fusion = f32[72,2048]{1,0:T(8,128)} fusion(f32[72,2048]{1,0:T(8,128)} %reshape.63784, f32[1024,1024]{0,1:T(8,128)} %get-tuple-element.171, f32[1024,1024]{0,1:T(8,128)} %get-tuple-element.170, f32[1024,1024]{0,1:T(8,128)} %get-tuple-element.169), kind=kOutput, calls=%fused_computation.39 | convolution fusion | flops 3636609024 | bytes 13762560 | tf_op jit(solution)/shard_map/rq,pq->rp/dot_general | solution.py:186
  (773 shorter events, 237.5 us)
Async XLA Ops:
  0.0 5.6 copy-start
  3.0 70.9 %collective-permute-start.1 = (f32[2,3,3,8,1024]{4,3,2,1,0:T(8,128)}, f32[2,3,3,8,1024]{4,3,2,1,0:T(8,128)S(1)}, u32[]{:S(2)}, u32[]{:S(2)}) collective-permute-start(f32[2,3,3,8,1024]{4,3,2,1,0:T(8,128)} %get-tuple-element.30), channel_id=1, source_target_pairs={{120,0},{0,8},{8,16},{16,24},{24,32},{32,40},{40,48},{48,56},{56,6... | collective-permute-start | bytes 1769480 | tf_op jit(solution)/shard_map/ppermute | solution.py:14
  6.3 67.6 %collective-permute-start = (f32[2,3,3,1,1024]{4,3,2,1,0:T(1,128)}, f32[2,3,3,1,1024]{4,3,2,1,0:T(1,128)}, u32[]{:S(2)}, u32[]{:S(2)}) collective-permute-start(f32[2,3,3,1,1024]{4,3,2,1,0:T(1,128)} %slice_bitcast_fusion.33), channel_id=1, source_target_pairs={{7,0},{0,1},{1,2},{2,3},{3,4},{4,5},{5,6},{6,7},{15,8},{8,9},{9,10... | collective-permute-start | bytes 221192 | tf_op jit(solution)/shard_map/ppermute | solution.py:14
  63.3 10.5 %copy-start.8 = (f32[2,3,3,1,8,1024]{5,4,2,1,0,3:T(8,128)S(1)}, f32[2,3,3,1,8,1024]{5,4,2,1,0,3:T(8,128)}, u32[]{:S(2)}) copy-start(f32[2,3,3,1,8,1024]{5,4,2,1,0,3:T(8,128)} %get-tuple-element.29) | copy-start | bytes 1769476
  63.3 10.6 %copy-start.9 = (f32[2,3,3,8,1023]{4,3,2,1,0:T(8,128)S(1)}, f32[2,3,3,8,1023]{4,3,2,1,0:T(8,128)}, u32[]{:S(2)}) copy-start(f32[2,3,3,8,1023]{4,3,2,1,0:T(8,128)} %slice_bitcast_fusion.3) | copy-start | bytes 1767748
  63.3 10.6 %copy-start.10 = (f32[2,3,3,8,993]{4,3,2,1,0:T(8,128)S(1)}, f32[2,3,3,8,993]{4,3,2,1,0:T(8,128)}, u32[]{:S(2)}) copy-start(f32[2,3,3,8,993]{4,3,2,1,0:T(8,128)} %slice_bitcast_fusion.4) | copy-start | bytes 1715908
  63.3 10.6 %copy-start.13 = (f32[2,3,3,8,31]{4,3,2,1,0:T(8,128)S(1)}, f32[2,3,3,8,31]{4,3,2,1,0:T(8,128)}, u32[]{:S(2)}) copy-start(f32[2,3,3,8,31]{4,3,2,1,0:T(8,128)} %slice_bitcast_fusion.32) | copy-start | bytes 53572
  63.4 10.6 %copy-start.14 = (f32[2,3,3,8,1]{4,3,2,1,0:T(8,128)S(1)}, f32[2,3,3,8,1]{4,3,2,1,0:T(8,128)}, u32[]{:S(2)}) copy-start(f32[2,3,3,8,1]{4,3,2,1,0:T(8,128)} %copy.2290) | copy-start | bytes 1732
  63.4 10.6 %copy-start.16 = (pred[1024]{0:T(1024)(128)(4,1)S(1)}, pred[1024]{0:T(1024)(128)(4,1)}, u32[]{:S(2)}) copy-start(pred[1024]{0:T(1024)(128)(4,1)} %broadcast_compare_fusion) | copy-start | bytes 3076
  73.7 6.0 copy-start.1
  74.0 2.4 copy-start.6
  111.2 22.0 %all-to-all-start = ((f32[16,1,9216]{2,1,0:T(1,128)}), f32[16,1,9216]{2,1,0:T(1,128)S(1)}, u32[]{:S(2)}, u32[]{:S(2)}) async-start(f32[16,1,9216]{2,1,0:T(1,128)} %reshape.64562), calls=%async_computation | async-start | bytes 1179648 | tf_op jit(solution)/shard_map/all_to_all | solution.py:225
  173.4 15.8 %all-to-all-start.1 = ((f32[8,1,18432]{2,1,0:T(1,128)}), f32[8,1,18432]{2,1,0:T(1,128)S(1)}, u32[]{:S(2)}, u32[]{:S(2)}) async-start(f32[8,1,18432]{2,1,0:T(1,128)} %reshape.64564), calls=%async_computation.1 | async-start | bytes 1179648 | tf_op jit(solution)/shard_map/all_to_all | solution.py:224
  254.8 21.5 %all-to-all-start.2 = ((f32[16,1,9216]{2,1,0:T(1,128)}), f32[16,1,9216]{2,1,0:T(1,128)}, u32[]{:S(2)}, u32[]{:S(2)}) async-start(f32[16,1,9216]{2,1,0:T(1,128)} %reshape.64566), calls=%async_computation.2 | async-start | bytes 1179648 | tf_op jit(solution)/shard_map/all_to_all | solution.py:244
  282.7 9.7 %copy-start.7 = (f32[2,3,3,8,1024]{4,3,2,1,0:T(8,128)S(1)}, f32[2,3,3,8,1024]{4,3,2,1,0:T(8,128)}, u32[]{:S(2)}) copy-start(f32[2,3,3,8,1024]{4,3,2,1,0:T(8,128)} %copy-done.6) | copy-start | bytes 1769476
  287.4 13.4 %all-to-all-start.3 = ((f32[8,1,18432]{2,1,0:T(1,128)}), f32[8,1,18432]{2,1,0:T(1,128)S(1)}, u32[]{:S(2)}, u32[]{:S(2)}) async-start(f32[8,1,18432]{2,1,0:T(1,128)} %reshape.64568), calls=%async_computation.3 | async-start | bytes 1179648 | tf_op jit(solution)/shard_map/all_to_all | solution.py:243
  346.0 3.0 copy-start.2
  346.0 3.0 copy-start.3
  346.2 8.1 %collective-permute-start.2 = (f32[2,3,3,1,8,1024]{5,4,1,2,3,0:T(8,128)S(1)}, f32[2,3,3,1,8,1024]{5,4,1,2,3,0:T(8,128)S(1)}, u32[]{:S(2)}, u32[]{:S(2)}) collective-permute-start(f32[2,3,3,1,8,1024]{5,4,1,2,3,0:T(8,128)S(1)} %pad_maximum_fusion), channel_id=1, source_target_pairs={{0,8},{8,16},{16,24},{24,32},{32,40},{40,48},{48,56},{56,64},{64,7... | collective-permute-start | bytes 1769480 | tf_op jit(solution)/shard_map/ppermute | solution.py:23
  347.3 10.0 %collective-permute-start.3 = (f32[2,3,3,1,8,1024]{5,4,1,2,3,0:T(8,128)S(1)}, f32[2,3,3,1,8,1024]{5,4,1,2,3,0:T(8,128)S(1)}, u32[]{:S(2)}, u32[]{:S(2)}) collective-permute-start(f32[2,3,3,1,8,1024]{5,4,1,2,3,0:T(8,128)S(1)} %pad_maximum_fusion), channel_id=1, source_target_pairs={{8,0},{16,8},{24,16},{32,24},{40,32},{48,40},{56,48},{64,56},{72,6... | collective-permute-start | bytes 1769480 | tf_op jit(solution)/shard_map/ppermute | solution.py:26
  357.6 4.9 collective-permute-start.5
  358.9 9.6 %collective-permute-start.4 = (f32[2,3,3,3,1,1024]{5,3,4,2,1,0:T(4,128)S(1)}, f32[2,3,3,3,1,1024]{5,3,4,2,1,0:T(4,128)S(1)}, u32[]{:S(2)}, u32[]{:S(2)}) collective-permute-start(f32[2,3,3,3,1,1024]{5,3,4,2,1,0:T(4,128)S(1)} %copy.3080), channel_id=1, source_target_pairs={{0,1},{1,2},{2,3},{3,4},{4,5},{5,6},{6,7},{7,0},{8,9},{9,10},{10,1... | collective-permute-start | bytes 663560 | tf_op jit(solution)/shard_map/ppermute | solution.py:23
  363.9 4.7 copy-start.11
  363.9 4.7 copy-start.12
  364.2 8.1 %slice-start = ((s8[16777216]{0:T(1024)(128)(4,1)}), s8[4194304]{0:T(1024)(128)(4,1)S(1)}, s32[]{:S(2)}) async-start(s8[16777216]{0:T(1024)(128)(4,1)} %bitcast.5415), calls=%async_computation.8 | async-start | bytes 8388608
  370.1 2.2 slice-start.1
  371.0 2.8 slice-start.2
  371.4 3.6 slice-start.3
  508.0 6.4 copy-start.15
  666.0 8.6 %collective-permute-start.6 = (f32[2,3,3,1,8,1024]{5,4,2,1,3,0:T(8,128)S(1)}, f32[2,3,3,1,8,1024]{5,4,2,1,3,0:T(8,128)S(1)}, u32[]{:S(2)}, u32[]{:S(2)}) collective-permute-start(f32[2,3,3,1,8,1024]{5,4,2,1,3,0:T(8,128)S(1)} %pad_maximum_fusion.1), channel_id=1, source_target_pairs={{0,8},{8,16},{16,24},{24,32},{32,40},{40,48},{48,56},{56,64},{64,7... | collective-permute-start | bytes 1769480 | tf_op jit(solution)/shard_map/ppermute | solution.py:23
  667.8 9.6 %collective-permute-start.7 = (f32[2,3,3,1,8,1024]{5,4,2,1,3,0:T(8,128)S(1)}, f32[2,3,3,1,8,1024]{5,4,2,1,3,0:T(8,128)S(1)}, u32[]{:S(2)}, u32[]{:S(2)}) collective-permute-start(f32[2,3,3,1,8,1024]{5,4,2,1,3,0:T(8,128)S(1)} %pad_maximum_fusion.1), channel_id=1, source_target_pairs={{8,0},{16,8},{24,16},{32,24},{40,32},{48,40},{56,48},{64,56},{72,6... | collective-permute-start | bytes 1769480 | tf_op jit(solution)/shard_map/ppermute | solution.py:26
  677.5 4.9 collective-permute-start.8
  (2 other events, 2.0 us)
where the time goes:
time: 697 us; the launch traced here: 686 us
  local copies, waits for them, and re-layouts  255 us (37%)
  matrix products  147 us (21%)
  other arithmetic  122 us (18%)
  blocking collectives  70.7 us (10%)
  waiting for transfers between devices  50.8 us (7%)
  starting transfers between devices  35.6 us (5%)
    unnamed x63, local copies, waits for them, and re-layouts  120 us
    dot_general x4, matrix products, forward_apply(): jnp.dot(rows, table, precision=lax.Precision.HIGHEST, preferred_element_t...  74.2 us
    dot_general x4, matrix products, backward_apply(): jnp.einsum('rq,pq->rp', rows, table, precision=lax.Precision.HIGHEST, pre...  72.5 us
    neg x2, other arithmetic, dense_table(): -sine_value  47.3 us
    concatenate x2, other arithmetic, dense_table(): jnp.concatenate([jnp.concatenate([cosine, -sine_value], axis=1), jnp.conc...  25.9 us
    all_to_all x4, local copies, waits for them, and re-layouts, smooth_field(): lax.all_to_all(lax.all_to_all(spectral, 'ta', split_axis=1, concat_axis=4...  25.3 us
    all_to_all x3, local copies, waits for them, and re-layouts, smooth_field(): lax.all_to_all(plane, 'ta', split_axis=4, concat_axis=1, tiled=True)  24 us
    all_to_all x1, blocking collectives, smooth_field(): lax.all_to_all(plane, 'ta', split_axis=4, concat_axis=1, tiled=True)  22.7 us
  transfers between devices with their start and end apart: 13, of which 9 were waited for; matrix products, arithmetic and copies ran while one was open for 14% of the time, Pallas kernels for 0%

commit v1 on v0

v1 whole, which is shorter than its diff:
```python
import functools

import jax
import jax.numpy as jnp
import ml_dtypes
import numpy as np
from jax import lax
from jax.experimental import pallas as pl
from jax.experimental.pallas import tpu as pltpu
from jax.sharding import PartitionSpec as P

LX = 32
LY = 32
LZ = 64
LT = 16
ITERS = 2
NTA = 16
NGZ = 8
DEVICES = NTA * NGZ
MESH = pl.DeviceIdType.MESH
F32 = jnp.float32
BF16 = jnp.bfloat16


def cas(angle):
    return np.cos(angle) + np.sin(angle)


def halves(table):
    high = table.astype(ml_dtypes.bfloat16)
    low = (table - high.astype(np.float64)).astype(ml_dtypes.bfloat16)
    return high, low


def plane_modes():
    wave_y = [k for k in range(LY) if k % 4 == 0]
    wave_y += [k for k in range(LY) if k % 4 == 2]
    wave_y += [k for k in range(LY) if k % 2 == 1]
    return np.repeat(np.array(wave_y), LX), np.tile(np.arange(LX), LY)


def plane_tables():
    ky, kx = plane_modes()
    b = np.repeat(np.arange(8), LX)
    x = np.tile(np.arange(LX), 8)
    along_x = cas(2 * np.pi * (kx[:, None] * x[None, :] % LX) / LX)
    phase = 2 * np.pi * (ky[:, None] * b[None, :] % LY) / LY
    plain = cas(phase) * along_x
    sign = np.where(ky % 4 == 1, 1.0, -1.0)[:, None]
    mirrored = sign * cas(-phase) * along_x
    even = plain[0:512]
    odd = np.concatenate([plain[512:], mirrored[512:]], axis=1)
    return halves(even) + halves(odd)


def line_tables():
    t = np.arange(LT)
    along_t = cas(2 * np.pi * (t[:, None] * t[None, :] % LT) / LT)
    zb = np.arange(8)
    waves = [np.cos(0 * zb), np.cos(np.pi * zb)]
    for k in (1, 2, 3):
        waves += [np.cos(2 * np.pi * k * zb / 8), np.sin(2 * np.pi * k * zb / 8)]
    waves = np.stack(waves)
    first = np.einsum("qz,kt->qktz", waves, along_t).reshape(128, 128)
    z8 = np.arange(8)
    second = np.zeros((4, 2, 2, 8, 8, 8, 16))
    depth = np.zeros((4, 16), np.int64)
    for pair in range(4):
        for j in range(16):
            k1 = (0, 4)[j // 8] if pair == 0 else (pair, 8 - pair)[j // 8]
            kz = k1 + 8 * (j % 8)
            depth[pair, j] = kz
            beta = 2 * np.pi * (kz * z8 % LZ) / LZ
            for f in range(8):
                for s in range(2):
                    if pair == 0:
                        second[pair, j // 8, s, f, :, f, j] = cas(beta)
                    else:
                        second[pair, 0, s, f, :, f, j] = cas(beta)
                        second[pair, 1, s, f, :, f, j] = (1.0 if j < 8 else -1.0) * cas(-beta)
    second = second.reshape(4, 256, 128)
    sine_t = 4 * np.sin(np.pi * t / LT) ** 2
    sine_z = 4 * np.sin(np.pi * depth / LZ) ** 2
    base = np.zeros((4, 8, 16, 8, 16))
    base += sine_t[None, None, :, None, None] + sine_z[:, None, None, None, :]
    return first, second, base.reshape(4, 128, 128).astype(np.float32)


def make_tables():
    even_hi, even_lo, odd_hi, odd_lo = plane_tables()
    first, second, base = line_tables()
    first_hi, first_lo = halves(first)
    back_hi, back_lo = halves(first.T)
    second_hi, second_lo = halves(second)
    turned_hi, turned_lo = halves(np.swapaxes(second, 1, 2))
    firsts = np.stack(
        [
            np.concatenate([first_hi, first_hi], axis=1),
            np.concatenate([first_lo, np.zeros_like(first_lo)], axis=1),
            np.concatenate([back_hi, back_hi], axis=1),
            np.concatenate([back_lo, np.zeros_like(back_lo)], axis=1),
        ]
    )
    seconds = np.concatenate([second_hi, second_lo], axis=2)
    turned = np.concatenate([turned_hi, turned_lo], axis=1)
    ky, kx = plane_modes()
    sine_xy = 4 * np.sin(np.pi * ky / LY) ** 2 + 4 * np.sin(np.pi * kx / LX) ** 2
    sine_xy = np.repeat(sine_xy[:, None], 128, axis=1).astype(np.float32)
    return even_hi, even_lo, odd_hi, odd_lo, firsts, seconds, turned, base, sine_xy


def split(value):
    high = value.astype(BF16)
    return high, (value - high.astype(F32)).astype(BF16)


def fields_of(link):
    imag_sum = link(1, 0, 0) + link(1, 1, 1) + link(1, 2, 2)
    third = imag_sum * (2.0 / 3.0)
    return [
        link(0, 0, 1) - link(0, 1, 0),
        link(1, 0, 1) + link(1, 1, 0),
        link(0, 0, 2) - link(0, 2, 0),
        link(1, 0, 2) + link(1, 2, 0),
        link(0, 1, 2) - link(0, 2, 1),
        link(1, 1, 2) + link(1, 2, 1),
        2.0 * link(1, 0, 0) - third,
        2.0 * link(1, 1, 1) - third,
    ]


def inverse_root(value):
    guess = lax.rsqrt(value)
    return guess * (1.5 - 0.5 * value * guess * guess)


def cross_row(first, second):
    out = []
    for position in range(3):
        follow, beyond = (position + 1) % 3, (position + 2) % 3
        fr, fi = first[follow]
        gr, gi = first[beyond]
        sr, si = second[beyond]
        tr, ti = second[follow]
        real = fr * sr - fi * si - (gr * tr - gi * ti)
        imag = gr * ti + gi * tr - (fr * si + fi * sr)
        out.append((real, imag))
    return out


def gauge_of(x):
    a, b, c, d, e, f, d0, d1 = x
    n01 = a * a + b * b
    n02 = c * c + d * d
    n12 = e * e + f * f
    both = d0 + d1
    s01r = -both * b - (c * e + d * f)
    s01i = both * a - (d * e - c * f)
    s02r = d1 * d + (a * e - b * f)
    s02i = (a * f + b * e) - d1 * c
    s12r = d0 * f - (a * c + b * d)
    s12i = (b * c - a * d) - d0 * e
    r0 = [(1.0 - 0.5 * (d0 * d0 + n01 + n02), d0), (a + 0.5 * s01r, b + 0.5 * s01i), (c + 0.5 * s02r, d + 0.5 * s02i)]
    r1 = [(0.5 * s01r - a, b - 0.5 * s01i), (1.0 - 0.5 * (d1 * d1 + n01 + n12), d1), (e + 0.5 * s12r, f + 0.5 * s12i)]

    def unit(row):
        total = None
        for real, imag in row:
            term = real * real + imag * imag
            total = term if total is None else total + term
        scale = inverse_root(total)
        return [(real * scale, imag * scale) for real, imag in row]

    u0 = unit(r0)
    pr = pi = None
    for (ur, ui), (vr, vi) in zip(u0, r1):
        tr, ti = ur * vr + ui * vi, ur * vi - ui * vr
        pr = tr if pr is None else pr + tr
        pi = ti if pi is None else pi + ti
    v = [(vr - (pr * ur - pi * ui), vi - (pr * ui + pi * ur)) for (ur, ui), (vr, vi) in zip(u0, r1)]
    u1 = unit(v)
    return [u0, u1, cross_row(u0, u1)]


def rotated_link(left, link, right):
    rows = []
    for i in range(2):
        product = []
        for k in range(3):
            real = imag = None
            for m in range(3):
                lr, li = left[i][m]
                ur, ui = link(0, m, k), link(1, m, k)
                tr, ti = lr * ur - li * ui, lr * ui + li * ur
                real = tr if real is None else real + tr
                imag = ti if imag is None else imag + ti
            product.append((real, imag))
        row = []
        for j in range(3):
            real = imag = None
            for k in range(3):
                pr, pi = product[k]
                gr, gi = right[j][k]
                tr, ti = pr * gr + pi * gi, pi * gr - pr * gi
                real = tr if real is None else real + tr
                imag = ti if imag is None else imag + ti
            row.append((real, imag))
        rows.append(row)
    rows.append(cross_row(rows[0], rows[1]))
    return rows


def hop_count(offset):
    return sum(min(v, 4 - v) for v in offset[:3]) + 0.1 * offset[3]


OFFSETS = sorted(
    [
        (dx, dy, dz, dc)
        for dy in range(4)
        for dz in range(4)
        for dx in range(4)
        for dc in range(2)
        if dx + dy + dz + dc > 0
    ],
    key=lambda o: -hop_count(o),
)


def target(offset):
    ta = lax.axis_index("ta")
    gz = lax.axis_index("gz")
    y = (2 * (ta // 8) + gz % 2 + offset[1]) % 4
    to_ta = (y // 2) * 8 + (((ta // 2) % 4 + offset[0]) % 4) * 2 + (ta % 2 + offset[3]) % 2
    to_gz = ((gz // 2 + offset[2]) % 4) * 2 + y % 2
    return to_ta, to_gz


def kernel(
    links_hbm,
    even_hi_hbm,
    even_lo_hbm,
    odd_hi_hbm,
    odd_lo_hbm,
    firsts_hbm,
    seconds_hbm,
    turned_hbm,
    base_hbm,
    sine_hbm,
    out_hbm,
    links,
    even_hi,
    even_lo,
    odd_hi,
    odd_lo,
    firsts,
    seconds,
    turned,
    weight,
    sine,
    delta,
    along_y,
    along_z,
    exchange,
    smooth,
    gauge,
    ahead,
    link_out,
    link_in,
    edge_out,
    edge_in,
    table_sem,
    load_sem,
    store_sem,
    send_sem,
    recv_sem,
    edge_send_sem,
    edge_recv_sem,
):
    ta = lax.axis_index("ta")
    gz = lax.axis_index("gz")
    me = ta * NGZ + gz
    after = {"gz": (gz + 1) % NGZ}
    before = {"gz": (gz + NGZ - 1) % NGZ}

    barrier = pltpu.get_barrier_semaphore()
    loads = []
    for mu in (1, 0, 3, 2):
        for ct in range(8):
            copy = pltpu.make_async_copy(
                links_hbm.at[mu, :, :, :, 0, :, pl.ds(ct * 128, 128)],
                links.at[mu, :, :, :, pl.ds(ct * 8, 8), :],
                load_sem.at[mu],
            )
            copy.start()
    tables = []
    pairs = [
        (even_hi_hbm, even_hi),
        (even_lo_hbm, even_lo),
        (odd_hi_hbm, odd_hi),
        (odd_lo_hbm, odd_lo),
        (firsts_hbm, firsts),
        (seconds_hbm, seconds),
        (turned_hbm, turned),
        (base_hbm, weight),
        (sine_hbm.at[pl.ds(pl.multiple_of(me * 8, 8), 8)], sine),
    ]
    for index, (source, place) in enumerate(pairs):
        copy = pltpu.make_async_copy(source, place, table_sem.at[index])
        copy.start()
        tables.append(copy)
    for offset in OFFSETS:
        to_ta, to_gz = target(offset)
        pl.semaphore_signal(barrier, inc=1, device_id={"ta": to_ta, "gz": to_gz}, device_id_type=MESH)

    lane = lax.broadcasted_iota(jnp.int32, (8, 128), 1)
    first_x = lane % LX == 0
    last_x = lane % LX == LX - 1
    low_96 = lane < 96
    low_32 = lane < 32

    def tile_of(ref, mu, row):
        def link(part, i, k):
            return ref[mu, part, i, k, pl.ds(row, 8), :]

        return link

    def before_x(tile):
        return jnp.where(first_x, pltpu.roll(tile, 97, 1), pltpu.roll(tile, 1, 1))

    def after_x(tile):
        return jnp.where(last_x, pltpu.roll(tile, 31, 1), pltpu.roll(tile, 127, 1))

    def row_of(ct):
        return pl.multiple_of(ct * 8, 8)

    def wide_row(ct):
        return pl.multiple_of(ct * 16, 16)

    def load_wait(mu):
        whole = links.at[mu]
        pltpu.make_async_copy(whole, whole, load_sem.at[mu]).wait()

    def spread_fields(ct):
        row = row_of(ct)
        for f, value in enumerate(fields_of(tile_of(links, 1, row))):
            along_y[f, pl.ds(row, 8), :] = value
        wide = wide_row(ct)
        for f, value in enumerate(fields_of(tile_of(links, 2, row))):
            along_z[f, pl.ds(wide + 8, 8), :] = value

    def gather_fields(ct):
        row = row_of(ct)
        wide = wide_row(ct)
        previous = pl.multiple_of(((ct + 7) % 8) * 8, 8)
        column = pl.multiple_of(ct * 128, 128)
        in_x = fields_of(tile_of(links, 0, row))
        for f in range(8):
            total = before_x(in_x[f]) - in_x[f]
            here = along_y[f, pl.ds(row, 8), :]
            total += pltpu.roll(jnp.where(low_96, here, along_y[f, pl.ds(previous, 8), :]), 32, 1) - here
            total += along_z[f, pl.ds(wide + 7, 8), :] - along_z[f, pl.ds(wide + 8, 8), :]
            delta[pl.ds(f * 8, 8), pl.ds(column, 128)] = total
        for f, value in enumerate(fields_of(tile_of(links, 3, row))):
            delta[pl.ds(64 + f * 8, 8), pl.ds(column, 128)] = value

    def each_tile(body):
        def step(ct, carry):
            body(ct)
            return carry

        lax.fori_loop(0, 8, step, 0)

    def exchange_start(slot):
        source = exchange.at[slot]
        place = exchange.at[slot + 1]
        mine = pl.ds(pl.multiple_of(me * 8, 8), 8)
        pltpu.make_async_copy(source.at[mine], place.at[mine], recv_sem.at[slot // 2]).start()
        for offset in OFFSETS:
            to_ta, to_gz = target(offset)
            chunk = pl.ds(pl.multiple_of((to_ta * NGZ + to_gz) * 8, 8), 8)
            pltpu.make_async_remote_copy(
                source.at[chunk],
                place.at[mine],
                send_sem.at[slot // 2],
                recv_sem.at[slot // 2],
                device_id={"ta": to_ta, "gz": to_gz},
                device_id_type=MESH,
            ).start()

    def exchange_wait(slot):
        whole = exchange.at[slot + 1]
        pltpu.make_async_copy(whole, whole, recv_sem.at[slot // 2]).wait()

    def exchange_sent(slot):
        part = exchange.at[slot, pl.ds(0, 1016)]
        pltpu.make_async_copy(part, part, send_sem.at[slot // 2]).wait()

    def product_nt(left_hi, left_lo, right):
        high, low = split(right)
        both = jnp.concatenate([high, low], axis=0)
        dims = (((1,), (1,)), ((), ()))
        wide = lax.dot_general(left_hi, both, dims, preferred_element_type=F32)
        return wide[:, 0:128] + wide[:, 128:256] + lax.dot_general(left_lo, high, dims, preferred_element_type=F32)

    def plane_forward(slot):
        x0, x1, x2, x3 = [delta[:, a * 256 : (a + 1) * 256] for a in range(4)]
        p, m, q, n = x0 + x2, x0 - x2, x1 + x3, x1 - x3
        exchange[slot, 0:256, :] = product_nt(even_hi[0:256, :], even_lo[0:256, :], p + q)
        exchange[slot, 256:512, :] = product_nt(even_hi[256:512, :], even_lo[256:512, :], p - q)
        exchange[slot, 512:1024, :] = product_nt(odd_hi[...], odd_lo[...], jnp.concatenate([m, n], axis=1))

    def product_tn(left, right_hi, right_lo):
        turned_left = jnp.concatenate(
            [left[i * 128 : (i + 1) * 128, :].T for i in range(left.shape[0] // 128)], axis=1
        )
        high, low = split(turned_left)
        tall = jnp.dot(jnp.concatenate([high, low], axis=0), right_hi, preferred_element_type=F32)
        return tall[0:128] + tall[128:256] + jnp.dot(high, right_lo, preferred_element_type=F32)

    def plane_backward(slot):
        b0 = product_tn(exchange[slot, 0:256, :], even_hi[0:256, :], even_lo[0:256, :])
        b2 = product_tn(exchange[slot, 256:512, :], even_hi[256:512, :], even_lo[256:512, :])
        odd = product_tn(exchange[slot, 512:1024, :], odd_hi[...], odd_lo[...])
        c, s = odd[:, 0:256], odd[:, 256:512]
        plus, minus = b0 + b2, b0 - b2
        for a, value in enumerate((plus + c, minus + s, plus - c, minus - s)):
            for side in range(2):
                ct = 2 * a + side
                for sf in range(16):
                    smooth[sf, ct * 8 : ct * 8 + 8, :] = value[sf * 8 : sf * 8 + 8, side * 128 : side * 128 + 128]

    tall_lane = lax.broadcasted_iota(jnp.int32, (128, 128), 1)
    in_space = tall_lane < 64

    def line_filter(slot):
        parts = []
        for j in range(8):
            got = exchange[slot, pl.ds(j, 128, stride=8), :]
            late = jnp.concatenate([got[120:128], got[0:120]], axis=0)
            parts.append(jnp.where(in_space, got, late - got))
        high, low = split(jnp.concatenate(parts, axis=1))
        stacked = jnp.concatenate([high, low], axis=0)
        lines = jnp.dot(firsts[0], stacked, preferred_element_type=F32)
        lines += jnp.dot(firsts[1, :, 0:128], high, preferred_element_type=F32)
        back = [[None] * 8 for _ in range(8)]
        for p in range(4):
            rows = []
            for j in range(8):
                rows.append(
                    jnp.concatenate(
                        [lines[p * 32 + h * 16 : p * 32 + h * 16 + 16, j * 128 : j * 128 + 128] for h in range(2)],
                        axis=1,
                    )
                )
            high, low = split(jnp.concatenate(rows, axis=0))
            wide = jnp.dot(high, seconds[p], preferred_element_type=F32)
            modes = wide[:, 0:128] + wide[:, 128:256]
            modes += jnp.dot(low, seconds[p, :, 0:128], preferred_element_type=F32)
            modes = modes * weight[p]
            high, low = split(modes)
            turn_hi = turned[p, 0:128, :]
            near = jnp.dot(high, turn_hi, preferred_element_type=F32)
            near += jnp.dot(low, turn_hi, preferred_element_type=F32)
            near += jnp.dot(high, turned[p, 128:256, :], preferred_element_type=F32)
            for j in range(8):
                for h in range(2):
                    back[2 * p + h][j] = near[j * 16 : j * 16 + 16, h * 128 : h * 128 + 128]
        high, low = split(jnp.concatenate([jnp.concatenate(row, axis=1) for row in back], axis=0))
        stacked = jnp.concatenate([high, low], axis=0)
        sites = jnp.dot(firsts[2], stacked, preferred_element_type=F32)
        sites += jnp.dot(firsts[3, :, 0:128], high, preferred_element_type=F32)
        for j in range(8):
            here = sites[:, j * 128 : j * 128 + 128]
            early = jnp.concatenate([here[8:128], here[0:8]], axis=0)
            exchange[slot + 1, pl.ds(j, 128, stride=8), :] = jnp.where(in_space, here, early)

    def store_gauge(ref, row, matrix):
        for i in range(3):
            for k in range(3):
                for part in range(2):
                    ref[part, i, k, pl.ds(row, 8), :] = matrix[i][k][part]

    def load_gauge(ref, window):
        return [[(ref[0, i, k, window, :], ref[1, i, k, window, :]) for k in range(3)] for i in range(3)]

    def make_gauge(ct):
        row = row_of(ct)
        store_gauge(gauge, wide_row(ct), gauge_of([smooth[f, pl.ds(row, 8), :] for f in range(8)]))
        store_gauge(ahead, row, gauge_of([smooth[8 + f, pl.ds(row, 8), :] for f in range(8)]))

    def store_link(mu, row, rows):
        for i in range(3):
            for k in range(3):
                for part in range(2):
                    links[mu, part, i, k, pl.ds(row, 8), :] = rows[i][k][part]

    def mapped(left, fn):
        return [[(fn(re), fn(im)) for re, im in row] for row in left]

    def rotate_xyt(ct):
        row = row_of(ct)
        left = load_gauge(gauge, pl.ds(wide_row(ct), 8))
        store_link(0, row, rotated_link(left, tile_of(links, 0, row), mapped(left, after_x)))
        following = load_gauge(gauge, pl.ds(pl.multiple_of(((ct + 1) % 8) * 16, 16), 8))
        right = [
            [
                tuple(pltpu.roll(jnp.where(low_32, following[i][k][part], left[i][k][part]), 96, 1) for part in range(2))
                for k in range(3)
            ]
            for i in range(3)
        ]
        store_link(1, row, rotated_link(left, tile_of(links, 1, row), right))
        store_link(3, row, rotated_link(left, tile_of(links, 3, row), load_gauge(ahead, pl.ds(row, 8))))

    def rotate_z(ct):
        row = row_of(ct)
        wide = wide_row(ct)
        left = load_gauge(gauge, pl.ds(wide, 8))
        right = load_gauge(gauge, pl.ds(wide + 1, 8))
        store_link(2, row, rotated_link(left, tile_of(links, 2, row), right))

    def edge_copy(way, device):
        return pltpu.make_async_remote_copy(
            edge_out.at[way], edge_in.at[way], edge_send_sem.at[way], edge_recv_sem.at[way], device_id=device,
            device_id_type=MESH,
        )

    load_wait(1)
    load_wait(2)
    for part in range(2):
        for i in range(3):
            for k in range(3):
                link_out[part, i, k] = links[2, part, i, k, pl.ds(7, 8, stride=8), :]
    each_tile(spread_fields)
    load_wait(0)
    load_wait(3)
    tables[7].wait()
    tables[8].wait()
    scale = 16.0 * 0.02 / (LX * LY * LZ * LT)
    for p in range(4):
        for j in range(8):
            total = weight[p, j * 16 : j * 16 + 16, :] + sine[j : j + 1, :]
            empty = total < 1e-6
            weight[p, j * 16 : j * 16 + 16, :] = jnp.where(empty, 0.0, scale / jnp.where(empty, 1.0, total))
    for index in range(7):
        tables[index].wait()
    pl.semaphore_wait(barrier, DEVICES - 1)
    link_copy = pltpu.make_async_remote_copy(
        link_out, link_in, edge_send_sem.at[4], edge_recv_sem.at[4], device_id=after, device_id_type=MESH
    )
    link_copy.start()
    link_copy.wait_recv()
    for f, value in enumerate(fields_of(lambda part, i, k: link_in[part, i, k])):
        along_z[f, pl.ds(7, 8, stride=16), :] = value

    for iteration in range(ITERS):
        last = iteration + 1 == ITERS
        slot = 4 * iteration
        each_tile(gather_fields)
        plane_forward(slot)
        exchange_start(slot)
        exchange_wait(slot)
        line_filter(slot + 1)
        exchange_start(slot + 2)
        exchange_wait(slot + 2)
        plane_backward(slot + 3)
        high_way, low_way = 2 * iteration, 2 * iteration + 1
        for f in range(8):
            edge_out[high_way, f] = smooth[f, pl.ds(0, 8, stride=8), :]
        to_before = edge_copy(high_way, before)
        to_before.start()
        if not last:
            for f in range(8):
                edge_out[low_way, f] = smooth[f, pl.ds(7, 8, stride=8), :]
            to_after = edge_copy(low_way, after)
            to_after.start()
        each_tile(make_gauge)
        each_tile(rotate_xyt)
        if last:
            for mu in (0, 1, 3):
                for ct in range(8):
                    pltpu.make_async_copy(
                        links.at[mu, :, :, :, pl.ds(ct * 8, 8), :],
                        out_hbm.at[mu, :, :, :, 0, :, pl.ds(ct * 128, 128)],
                        store_sem.at[mu],
                    ).start()
        to_before.wait_recv()
        halo = gauge_of([edge_in[high_way, f] for f in range(8)])
        for part in range(2):
            for i in range(3):
                for k in range(3):
                    gauge[part, i, k, pl.ds(8, 8, stride=16), :] = halo[i][k][part]
        each_tile(rotate_z)
        if last:
            for ct in range(8):
                pltpu.make_async_copy(
                    links.at[2, :, :, :, pl.ds(ct * 8, 8), :],
                    out_hbm.at[2, :, :, :, 0, :, pl.ds(ct * 128, 128)],
                    store_sem.at[2],
                ).start()
        else:
            to_after.wait_recv()
            left = gauge_of([edge_in[low_way, f] for f in range(8)])
            right = load_gauge(gauge, pl.ds(0, 8, stride=16))
            below = rotated_link(left, lambda part, i, k: link_in[part, i, k], right)
            each_tile(spread_fields)
            for f, value in enumerate(fields_of(lambda part, i, k: below[i][k][part])):
                along_z[f, pl.ds(7, 8, stride=16), :] = value
            to_after.wait_send()
        to_before.wait_send()

    link_copy.wait_send()
    for slot in range(0, 4 * ITERS, 2):
        exchange_sent(slot)
    for mu in range(4):
        whole = links.at[mu]
        pltpu.make_async_copy(whole, whole, store_sem.at[mu]).wait()


def on_device(gauge_links):
    tables = make_tables()
    operands = [jnp.asarray(table) for table in tables]
    anywhere = pl.BlockSpec(memory_space=pl.ANY)
    scratch = [
        pltpu.VMEM((4, 2, 3, 3, 64, 128), F32),
        pltpu.VMEM((512, 256), BF16),
        pltpu.VMEM((512, 256), BF16),
        pltpu.VMEM((512, 512), BF16),
        pltpu.VMEM((512, 512), BF16),
        pltpu.VMEM((4, 128, 256), BF16),
        pltpu.VMEM((4, 256, 256), BF16),
        pltpu.VMEM((4, 256, 256), BF16),
        pltpu.VMEM((4, 128, 128), F32),
        pltpu.VMEM((8, 128), F32),
        pltpu.VMEM((128, 1024), F32),
        pltpu.VMEM((8, 64, 128), F32),
        pltpu.VMEM((8, 128, 128), F32),
        pltpu.VMEM((4 * ITERS, 1024, 128), F32),
        pltpu.VMEM((16, 64, 128), F32),
        pltpu.VMEM((2, 3, 3, 128, 128), F32),
        pltpu.VMEM((2, 3, 3, 64, 128), F32),
        pltpu.VMEM((2, 3, 3, 8, 128), F32),
        pltpu.VMEM((2, 3, 3, 8, 128), F32),
        pltpu.VMEM((4, 8, 8, 128), F32),
        pltpu.VMEM((4, 8, 8, 128), F32),
        pltpu.SemaphoreType.DMA((9,)),
        pltpu.SemaphoreType.DMA((4,)),
        pltpu.SemaphoreType.DMA((4,)),
        pltpu.SemaphoreType.DMA((2 * ITERS,)),
        pltpu.SemaphoreType.DMA((2 * ITERS,)),
        pltpu.SemaphoreType.DMA((5,)),
        pltpu.SemaphoreType.DMA((5,)),
    ]
    return pl.pallas_call(
        kernel,
        out_shape=jax.ShapeDtypeStruct(gauge_links.shape, F32),
        in_specs=[anywhere] * (1 + len(operands)),
        out_specs=anywhere,
        scratch_shapes=scratch,
        compiler_params=pltpu.CompilerParams(
            collective_id=0, has_side_effects=True, vmem_limit_bytes=48 * 1024 * 1024
        ),
    )(gauge_links, *operands)


def solution(mesh):
    specs = P(None, None, None, None, "ta", "gz", None)
    return jax.shard_map(on_device, mesh=mesh, in_specs=(specs,), out_specs=specs, check_vma=False)
```

time: 697 us -> 73.2 us (0.11); the launches traced: 686 us -> 72.6 us
  local copies, waits for them, and re-layouts: 255 us -> 10.4 us
  matrix products: 147 us -> 0 us
  other arithmetic: 122 us -> 0 us
  blocking collectives: 70.7 us -> 0 us
  Pallas kernels: 0 us -> 62.2 us
  waiting for transfers between devices: 50.8 us -> 0 us
  starting transfers between devices: 35.6 us -> 0 us
    dot_general x8 -> x0, matrix products: 147 us -> none  [the longest x4 74.2 us: forward_apply(): jnp.dot(rows, table, precision=lax.Precision.HIGHEST, preferred_element_t...]
    unnamed x63 -> x19, local copies, waits for them, and re-layouts: 120 us -> 10.4 us
    all_to_all x15 -> x0, local copies, waits for them, and re-layouts: 71.9 us -> none  [the longest x4 25.3 us: smooth_field(): lax.all_to_all(lax.all_to_all(spectral, 'ta', split_axis=1, concat_axis=4...]
    all_to_all x4 -> x0, blocking collectives: 70.7 us -> none  [the longest x1 22.7 us: smooth_field(): lax.all_to_all(plane, 'ta', split_axis=4, concat_axis=1, tiled=True)]
    pallas_call x0 -> x1, Pallas kernels: none -> 62.2 us  [on_device(): pl.pallas_call(kernel, out_shape=jax.ShapeDtypeStruct(gauge_links.shape,...]
    neg x8 -> x0, other arithmetic: 47.7 us -> none  [the longest x2 47.3 us: dense_table(): -sine_value]
    all_to_all x4 -> x0, waiting for transfers between devices: 28.9 us -> none  [the longest x1 11 us: smooth_field(): lax.all_to_all(spectral, 'ta', split_axis=1, concat_axis=4, tiled=True)]
    concatenate x5 -> x0, other arithmetic: 26.2 us -> none  [the longest x2 25.9 us: dense_table(): jnp.concatenate([jnp.concatenate([cosine, -sine_value], axis=1), jnp.conc...]
  transfers between devices with their start and end apart: 13 -> 0, of which waited for: 9 -> 0; matrix products, arithmetic and copies ran while one was open for 14% -> 0% of each run, Pallas kernels for 0% -> 0%
where the time goes in v1:
time: 73.2 us; the launch traced here: 72.6 us
  Pallas kernels  62.2 us (85%)
  local copies, waits for them, and re-layouts  10.4 us (14%)
    pallas_call x1, Pallas kernels, on_device(): pl.pallas_call(kernel, out_shape=jax.ShapeDtypeStruct(gauge_links.shape,...  62.2 us
    unnamed x19, local copies, waits for them, and re-layouts  10.4 us

profile of v1, /device:TPU:1, one launch (start us, length us, event | category | flops | bytes accessed | tf_op | source)
XLA Modules:
  0.0 72.6 jit_solution(5512254661980313185)
XLA Ops:
  0.0 0.0 copy-start
  0.0 1.0 %copy-done = f32[1024,128]{1,0:T(8,128)S(1)} copy-done((f32[1024,128]{1,0:T(8,128)S(1)}, f32[1024,128]{1,0:T(8,128)}, u32[]{:S(2)}) %copy-start) | copy-done | bytes 524312
  1.0 0.0 copy-start.1
  1.0 1.0 %copy-done.1 = bf16[4,256,256]{2,1,0:T(8,128)(2,1)S(1)} copy-done((bf16[4,256,256]{2,1,0:T(8,128)(2,1)S(1)}, bf16[4,256,256]{2,1,0:T(8,128)(2,1)}, u32[]{:S(2)}) %copy-start.1) | copy-done | bytes 524312
  2.1 0.0 copy-start.2
  2.1 1.0 %copy-done.2 = bf16[4,256,256]{2,1,0:T(8,128)(2,1)S(1)} copy-done((bf16[4,256,256]{2,1,0:T(8,128)(2,1)S(1)}, bf16[4,256,256]{2,1,0:T(8,128)(2,1)}, u32[]{:S(2)}) %copy-start.2) | copy-done | bytes 524312
  3.1 0.0 copy-start.3
  3.1 1.0 %copy-done.3 = bf16[512,512]{1,0:T(8,128)(2,1)S(1)} copy-done((bf16[512,512]{1,0:T(8,128)(2,1)S(1)}, bf16[512,512]{1,0:T(8,128)(2,1)}, u32[]{:S(2)}) %copy-start.3) | copy-done | bytes 524312
  4.2 0.0 copy-start.4
  4.2 1.0 %copy-done.4 = bf16[512,512]{1,0:T(8,128)(2,1)S(1)} copy-done((bf16[512,512]{1,0:T(8,128)(2,1)S(1)}, bf16[512,512]{1,0:T(8,128)(2,1)}, u32[]{:S(2)}) %copy-start.4) | copy-done | bytes 524312
  5.2 0.0 copy-start.5
  5.2 0.9 %copy-done.5 = f32[4,128,128]{2,1,0:T(8,128)S(1)} copy-done((f32[4,128,128]{2,1,0:T(8,128)S(1)}, f32[4,128,128]{2,1,0:T(8,128)}, u32[]{:S(2)}) %copy-start.5) | copy-done | bytes 262168
  6.2 0.0 copy-start.6
  6.2 0.9 %copy-done.6 = bf16[4,128,256]{2,1,0:T(8,128)(2,1)S(1)} copy-done((bf16[4,128,256]{2,1,0:T(8,128)(2,1)S(1)}, bf16[4,128,256]{2,1,0:T(8,128)(2,1)}, u32[]{:S(2)}) %copy-start.6) | copy-done | bytes 262168
  7.1 0.0 copy-start.7
  7.1 0.9 %copy-done.7 = bf16[512,256]{1,0:T(8,128)(2,1)S(1)} copy-done((bf16[512,256]{1,0:T(8,128)(2,1)S(1)}, bf16[512,256]{1,0:T(8,128)(2,1)}, u32[]{:S(2)}) %copy-start.7) | copy-done | bytes 262168
  8.1 0.0 copy-start.8
  8.1 0.9 %copy-done.8 = bf16[512,256]{1,0:T(8,128)(2,1)S(1)} copy-done((bf16[512,256]{1,0:T(8,128)(2,1)S(1)}, bf16[512,256]{1,0:T(8,128)(2,1)}, u32[]{:S(2)}) %copy-start.8) | copy-done | bytes 262168
  9.0 62.2 %shard_map.100 = f32[4,2,3,3,1,8,1024]{6,5,4,3,2,1,0:T(8,128)S(1)} custom-call(f32[4,2,3,3,1,8,1024]{6,5,4,3,2,1,0:T(8,128)} %links_hbm.1, bf16[512,256]{1,0:T(8,128)(2,1)S(1)} %copy-done.8, bf16[512,256]{1,0:T(8,128)(2,1)S(1)} %copy-done.7, bf16[512,512]{1,0:T(8,128)(2,1)S(1)} %copy-done.4, bf16[512,512]{1,0:T(8,128)(2,1)S(1)} %copy-done.3, ...), custom_call_target="tpu_custom_call" | custom-call | tf_op jit(solution)/shard_map/pallas_call | solution.py:655
  71.2 1.4 %copy.12 = f32[4,2,3,3,1,8,1024]{6,5,4,3,2,1,0:T(8,128)} copy(f32[4,2,3,3,1,8,1024]{6,5,4,3,2,1,0:T(8,128)S(1)} %shard_map.100) | data formatting | bytes 4718592
Async XLA Ops:
  0.0 1.0 %copy-start = (f32[1024,128]{1,0:T(8,128)S(1)}, f32[1024,128]{1,0:T(8,128)}, u32[]{:S(2)}) copy-start(f32[1024,128]{1,0:T(8,128)} %constant.26.clone.sine_hbm) | copy-start | bytes 1572868
  1.0 1.0 %copy-start.1 = (bf16[4,256,256]{2,1,0:T(8,128)(2,1)S(1)}, bf16[4,256,256]{2,1,0:T(8,128)(2,1)}, u32[]{:S(2)}) copy-start(bf16[4,256,256]{2,1,0:T(8,128)(2,1)} %constant.24.clone.turned_hbm) | copy-start | bytes 1572868
  2.1 1.0 %copy-start.2 = (bf16[4,256,256]{2,1,0:T(8,128)(2,1)S(1)}, bf16[4,256,256]{2,1,0:T(8,128)(2,1)}, u32[]{:S(2)}) copy-start(bf16[4,256,256]{2,1,0:T(8,128)(2,1)} %constant.23.clone.seconds_hbm) | copy-start | bytes 1572868
  3.1 1.0 %copy-start.3 = (bf16[512,512]{1,0:T(8,128)(2,1)S(1)}, bf16[512,512]{1,0:T(8,128)(2,1)}, u32[]{:S(2)}) copy-start(bf16[512,512]{1,0:T(8,128)(2,1)} %constant.21.clone.odd_lo_hbm) | copy-start | bytes 1572868
  4.2 1.0 %copy-start.4 = (bf16[512,512]{1,0:T(8,128)(2,1)S(1)}, bf16[512,512]{1,0:T(8,128)(2,1)}, u32[]{:S(2)}) copy-start(bf16[512,512]{1,0:T(8,128)(2,1)} %constant.20.clone.odd_hi_hbm) | copy-start | bytes 1572868
  5.2 0.9 %copy-start.5 = (f32[4,128,128]{2,1,0:T(8,128)S(1)}, f32[4,128,128]{2,1,0:T(8,128)}, u32[]{:S(2)}) copy-start(f32[4,128,128]{2,1,0:T(8,128)} %constant.25.clone.base_hbm) | copy-start | bytes 786436
  6.2 0.9 %copy-start.6 = (bf16[4,128,256]{2,1,0:T(8,128)(2,1)S(1)}, bf16[4,128,256]{2,1,0:T(8,128)(2,1)}, u32[]{:S(2)}) copy-start(bf16[4,128,256]{2,1,0:T(8,128)(2,1)} %constant.22.clone.firsts_hbm) | copy-start | bytes 786436
  7.1 0.9 %copy-start.7 = (bf16[512,256]{1,0:T(8,128)(2,1)S(1)}, bf16[512,256]{1,0:T(8,128)(2,1)}, u32[]{:S(2)}) copy-start(bf16[512,256]{1,0:T(8,128)(2,1)} %constant.19.clone.even_lo_hbm) | copy-start | bytes 786436
  8.1 0.9 %copy-start.8 = (bf16[512,256]{1,0:T(8,128)(2,1)S(1)}, bf16[512,256]{1,0:T(8,128)(2,1)}, u32[]{:S(2)}) copy-start(bf16[512,256]{1,0:T(8,128)(2,1)} %constant.18.clone.even_hi_hbm) | copy-start | bytes 786436

commit v2 on v1

--- a/solution.py
+++ b/solution.py
@@ -17,6 +17,7 @@
 NTA = 16
 NGZ = 8
 DEVICES = NTA * NGZ
+SPARE_ROWS = 16384
 MESH = pl.DeviceIdType.MESH
 F32 = jnp.float32
 BF16 = jnp.bfloat16
@@ -87,7 +88,7 @@
 
 
 def make_tables():
-    even_hi, even_lo, odd_hi, odd_lo = plane_tables()
+    plane = plane_tables()
     first, second, base = line_tables()
     first_hi, first_lo = halves(first)
     back_hi, back_lo = halves(first.T)
@@ -103,10 +104,16 @@
     )
     seconds = np.concatenate([second_hi, second_lo], axis=2)
     turned = np.concatenate([turned_hi, turned_lo], axis=1)
+    blocks = [plane[0], plane[1]]
+    for part in (plane[2], plane[3]):
+        blocks += [part[:, 0:256], part[:, 256:512]]
+    blocks += [firsts.reshape(512, 256), seconds.reshape(1024, 256), turned.reshape(1024, 256)]
     ky, kx = plane_modes()
     sine_xy = 4 * np.sin(np.pi * ky / LY) ** 2 + 4 * np.sin(np.pi * kx / LX) ** 2
     sine_xy = np.repeat(sine_xy[:, None], 128, axis=1).astype(np.float32)
-    return even_hi, even_lo, odd_hi, odd_lo, firsts, seconds, turned, base, sine_xy
+    tables = np.concatenate(blocks)
+    waves = np.concatenate([base.reshape(512, 128), sine_xy])
+    return np.resize(tables, (SPARE_ROWS, 256)), np.resize(waves, (SPARE_ROWS, 128))
 
 
 def split(value):
@@ -238,24 +245,11 @@
 
 def kernel(
     links_hbm,
-    even_hi_hbm,
-    even_lo_hbm,
-    odd_hi_hbm,
-    odd_lo_hbm,
-    firsts_hbm,
-    seconds_hbm,
-    turned_hbm,
-    base_hbm,
-    sine_hbm,
+    tables_hbm,
+    waves_hbm,
     out_hbm,
     links,
-    even_hi,
-    even_lo,
-    odd_hi,
-    odd_lo,
-    firsts,
-    seconds,
-    turned,
+    tables,
     weight,
     sine,
     delta,
@@ -269,6 +263,11 @@
     link_in,
     edge_out,
     edge_in,
+    edge,
+    edge_modes,
+    row_out,
+    row_in,
+    row_sem,
     table_sem,
     load_sem,
     store_sem,
@@ -293,22 +292,13 @@
                 load_sem.at[mu],
             )
             copy.start()
-    tables = []
-    pairs = [
-        (even_hi_hbm, even_hi),
-        (even_lo_hbm, even_lo),
-        (odd_hi_hbm, odd_hi),
-        (odd_lo_hbm, odd_lo),
-        (firsts_hbm, firsts),
-        (seconds_hbm, seconds),
-        (turned_hbm, turned),
-        (base_hbm, weight),
-        (sine_hbm.at[pl.ds(pl.multiple_of(me * 8, 8), 8)], sine),
+    table_copies = [
+        pltpu.make_async_copy(waves_hbm.at[pl.ds(0, 512)], weight, table_sem.at[0]),
+        pltpu.make_async_copy(waves_hbm.at[pl.ds(pl.multiple_of(512 + me * 8, 8), 8)], sine, table_sem.at[1]),
+        pltpu.make_async_copy(tables_hbm.at[pl.ds(0, 5632)], tables, table_sem.at[2]),
     ]
-    for index, (source, place) in enumerate(pairs):
-        copy = pltpu.make_async_copy(source, place, table_sem.at[index])
+    for copy in table_copies:
         copy.start()
-        tables.append(copy)
     for offset in OFFSETS:
         to_ta, to_gz = target(offset)
         pl.semaphore_signal(barrier, inc=1, device_id={"ta": to_ta, "gz": to_gz}, device_id_type=MESH)
@@ -348,6 +338,16 @@
         wide = wide_row(ct)
         for f, value in enumerate(fields_of(tile_of(links, 2, row))):
             along_z[f, pl.ds(wide + 8, 8), :] = value
+
+    top_row = lax.broadcasted_iota(jnp.int32, (8, 128), 0) == 0
+
+    def edge_fields(ct):
+        wide = wide_row(ct)
+        column = pl.ds(pl.multiple_of(ct * 128, 128), 128)
+        for f in range(8):
+            tile = along_z[f, pl.ds(wide + 8, 8), :]
+            edge[pl.ds(f * 8, 8), column] = jnp.where(top_row, pltpu.roll(tile, 1, 0), 0.0)
+            edge[pl.ds(64 + f * 8, 8), column] = jnp.zeros((8, 128), F32)
 
     def gather_fields(ct):
         row = row_of(ct)
@@ -371,7 +371,7 @@
 
         lax.fori_loop(0, 8, step, 0)
 
-    def exchange_start(slot):
+    def exchange_start(slot, with_rows=False):
         source = exchange.at[slot]
         place = exchange.at[slot + 1]
         mine = pl.ds(pl.multiple_of(me * 8, 8), 8)
@@ -387,6 +387,17 @@
                 device_id={"ta": to_ta, "gz": to_gz},
                 device_id_type=MESH,
             ).start()
+            if with_rows:
+                pltpu.make_async_remote_copy(
+                    row_out.at[to_ta * NGZ + to_gz],
+                    row_in.at[me],
+                    row_sem.at[0],
+                    row_sem.at[1],
+                    device_id={"ta": to_ta, "gz": to_gz},
+                    device_id_type=MESH,
+                ).start()
+        if with_rows:
+            pltpu.make_async_copy(row_out.at[me], row_in.at[me], row_sem.at[1]).start()
 
     def exchange_wait(slot):
         whole = exchange.at[slot + 1]
@@ -395,6 +406,13 @@
     def exchange_sent(slot):
         part = exchange.at[slot, pl.ds(0, 1016)]
         pltpu.make_async_copy(part, part, send_sem.at[slot // 2]).wait()
+
+    def table(first, count, columns=256):
+        return tables[first : first + count, 0:columns]
+
+    def odd_table(part):
+        first = 1024 + 1024 * part
+        return jnp.concatenate([table(first, 512), table(first + 512, 512)], axis=1)
 
     def product_nt(left_hi, left_lo, right):
         high, low = split(right)
@@ -403,12 +421,12 @@
         wide = lax.dot_general(left_hi, both, dims, preferred_element_type=F32)
         return wide[:, 0:128] + wide[:, 128:256] + lax.dot_general(left_lo, high, dims, preferred_element_type=F32)
 
-    def plane_forward(slot):
-        x0, x1, x2, x3 = [delta[:, a * 256 : (a + 1) * 256] for a in range(4)]
+    def plane_forward(source, place):
+        x0, x1, x2, x3 = [source[:, a * 256 : (a + 1) * 256] for a in range(4)]
         p, m, q, n = x0 + x2, x0 - x2, x1 + x3, x1 - x3
-        exchange[slot, 0:256, :] = product_nt(even_hi[0:256, :], even_lo[0:256, :], p + q)
-        exchange[slot, 256:512, :] = product_nt(even_hi[256:512, :], even_lo[256:512, :], p - q)
-        exchange[slot, 512:1024, :] = product_nt(odd_hi[...], odd_lo[...], jnp.concatenate([m, n], axis=1))
+        place[0:256, :] = product_nt(table(0, 256), table(512, 256), p + q)
+        place[256:512, :] = product_nt(table(256, 256), table(768, 256), p - q)
+        place[512:1024, :] = product_nt(odd_table(0), odd_table(1), jnp.concatenate([m, n], axis=1))
 
     def product_tn(left, right_hi, right_lo):
         turned_left = jnp.concatenate(
@@ -419,9 +437,9 @@
         return tall[0:128] + tall[128:256] + jnp.dot(high, right_lo, preferred_element_type=F32)
 
     def plane_backward(slot):
-        b0 = product_tn(exchange[slot, 0:256, :], even_hi[0:256, :], even_lo[0:256, :])
-        b2 = product_tn(exchange[slot, 256:512, :], even_hi[256:512, :], even_lo[256:512, :])
-        odd = product_tn(exchange[slot, 512:1024, :], odd_hi[...], odd_lo[...])
+        b0 = product_tn(exchange[slot, 0:256, :], table(0, 256), table(512, 256))
+        b2 = product_tn(exchange[slot, 256:512, :], table(256, 256), table(768, 256))
+        odd = product_tn(exchange[slot, 512:1024, :], odd_table(0), odd_table(1))
         c, s = odd[:, 0:256], odd[:, 256:512]
         plus, minus = b0 + b2, b0 - b2
         for a, value in enumerate((plus + c, minus + s, plus - c, minus - s)):
@@ -433,16 +451,30 @@
     tall_lane = lax.broadcasted_iota(jnp.int32, (128, 128), 1)
     in_space = tall_lane < 64
 
-    def line_filter(slot):
+    row_start = in_space & (tall_lane % 8 == 0)
+
+    def pack_rows():
+        total = edge_modes[pl.ds(0, 128, stride=8), :]
+        for j in range(1, 8):
+            total += pltpu.roll(edge_modes[pl.ds(j, 128, stride=8), :], j, 1)
+        row_out[...] = total.reshape(128, 1, 128)
+
+    def line_filter(slot, with_rows=False):
         parts = []
+        if with_rows:
+            rows = row_in[...].reshape(16, 8, 128)
+            rows = pltpu.roll(rows, 1, 1).reshape(128, 128)
         for j in range(8):
             got = exchange[slot, pl.ds(j, 128, stride=8), :]
             late = jnp.concatenate([got[120:128], got[0:120]], axis=0)
-            parts.append(jnp.where(in_space, got, late - got))
+            part = jnp.where(in_space, got, late - got)
+            if with_rows:
+                part += jnp.where(row_start, pltpu.roll(rows, 128 - j, 1) if j else rows, 0.0)
+            parts.append(part)
         high, low = split(jnp.concatenate(parts, axis=1))
         stacked = jnp.concatenate([high, low], axis=0)
-        lines = jnp.dot(firsts[0], stacked, preferred_element_type=F32)
-        lines += jnp.dot(firsts[1, :, 0:128], high, preferred_element_type=F32)
+        lines = jnp.dot(table(3072, 128), stacked, preferred_element_type=F32)
+        lines += jnp.dot(table(3200, 128, 128), high, preferred_element_type=F32)
         back = [[None] * 8 for _ in range(8)]
         for p in range(4):
             rows = []
@@ -454,22 +486,22 @@
                     )
                 )
             high, low = split(jnp.concatenate(rows, axis=0))
-            wide = jnp.dot(high, seconds[p], preferred_element_type=F32)
+            wide = jnp.dot(high, table(3584 + 256 * p, 256), preferred_element_type=F32)
             modes = wide[:, 0:128] + wide[:, 128:256]
-            modes += jnp.dot(low, seconds[p, :, 0:128], preferred_element_type=F32)
-            modes = modes * weight[p]
+            modes += jnp.dot(low, table(3584 + 256 * p, 256, 128), preferred_element_type=F32)
+            modes = modes * weight[p * 128 : p * 128 + 128, :]
             high, low = split(modes)
-            turn_hi = turned[p, 0:128, :]
+            turn_hi = table(4608 + 256 * p, 128)
             near = jnp.dot(high, turn_hi, preferred_element_type=F32)
             near += jnp.dot(low, turn_hi, preferred_element_type=F32)
-            near += jnp.dot(high, turned[p, 128:256, :], preferred_element_type=F32)
+            near += jnp.dot(high, table(4736 + 256 * p, 128), preferred_element_type=F32)
             for j in range(8):
                 for h in range(2):
                     back[2 * p + h][j] = near[j * 16 : j * 16 + 16, h * 128 : h * 128 + 128]
         high, low = split(jnp.concatenate([jnp.concatenate(row, axis=1) for row in back], axis=0))
         stacked = jnp.concatenate([high, low], axis=0)
-        sites = jnp.dot(firsts[2], stacked, preferred_element_type=F32)
-        sites += jnp.dot(firsts[3, :, 0:128], high, preferred_element_type=F32)
+        sites = jnp.dot(table(3328, 128), stacked, preferred_element_type=F32)
+        sites += jnp.dot(table(3456, 128, 128), high, preferred_element_type=F32)
         for j in range(8):
             here = sites[:, j * 128 : j * 128 + 128]
             early = jnp.concatenate([here[8:128], here[0:8]], axis=0)
@@ -535,33 +567,40 @@
     each_tile(spread_fields)
     load_wait(0)
     load_wait(3)
-    tables[7].wait()
-    tables[8].wait()
+    table_copies[0].wait()
+    table_copies[1].wait()
     scale = 16.0 * 0.02 / (LX * LY * LZ * LT)
     for p in range(4):
         for j in range(8):
-            total = weight[p, j * 16 : j * 16 + 16, :] + sine[j : j + 1, :]
+            total = weight[p * 128 + j * 16 : p * 128 + j * 16 + 16, :] + sine[j : j + 1, :]
             empty = total < 1e-6
-            weight[p, j * 16 : j * 16 + 16, :] = jnp.where(empty, 0.0, scale / jnp.where(empty, 1.0, total))
-    for index in range(7):
-        tables[index].wait()
+            weight[p * 128 + j * 16 : p * 128 + j * 16 + 16, :] = jnp.where(empty, 0.0, scale / jnp.where(empty, 1.0, total))
+    table_copies[2].wait()
+    for f in range(8):
+        along_z[f, pl.ds(7, 8, stride=16), :] = jnp.zeros((8, 128), F32)
+    each_tile(gather_fields)
+    each_tile(edge_fields)
+    plane_forward(edge, edge_modes)
+    pack_rows()
+    plane_forward(delta, exchange.at[0])
     pl.semaphore_wait(barrier, DEVICES - 1)
+    exchange_start(0, True)
     link_copy = pltpu.make_async_remote_copy(
         link_out, link_in, edge_send_sem.at[4], edge_recv_sem.at[4], device_id=after, device_id_type=MESH
     )
     link_copy.start()
-    link_copy.wait_recv()
-    for f, value in enumerate(fields_of(lambda part, i, k: link_in[part, i, k])):
-        along_z[f, pl.ds(7, 8, stride=16), :] = value
 
     for iteration in range(ITERS):
         last = iteration + 1 == ITERS
         slot = 4 * iteration
-        each_tile(gather_fields)
-        plane_forward(slot)
-        exchange_start(slot)
+        if iteration > 0:
+            each_tile(gather_fields)
+            plane_forward(delta, exchange.at[slot])
+            exchange_start(slot)
+        else:
+            pltpu.make_async_copy(row_in, row_in, row_sem.at[1]).wait()
         exchange_wait(slot)
-        line_filter(slot + 1)
+        line_filter(slot + 1, iteration == 0)
         exchange_start(slot + 2)
         exchange_wait(slot + 2)
         plane_backward(slot + 3)
@@ -601,6 +640,7 @@
                 ).start()
         else:
             to_after.wait_recv()
+            link_copy.wait_recv()
             left = gauge_of([edge_in[low_way, f] for f in range(8)])
             right = load_gauge(gauge, pl.ds(0, 8, stride=16))
             below = rotated_link(left, lambda part, i, k: link_in[part, i, k], right)
@@ -611,6 +651,7 @@
         to_before.wait_send()
 
     link_copy.wait_send()
+    pltpu.make_async_copy(row_out.at[pl.ds(0, 127)], row_out.at[pl.ds(0, 127)], row_sem.at[0]).wait()
     for slot in range(0, 4 * ITERS, 2):
         exchange_sent(slot)
     for mu in range(4):
@@ -619,19 +660,12 @@
 
 
 def on_device(gauge_links):
-    tables = make_tables()
-    operands = [jnp.asarray(table) for table in tables]
+    operands = [jnp.asarray(table) for table in make_tables()]
     anywhere = pl.BlockSpec(memory_space=pl.ANY)
     scratch = [
         pltpu.VMEM((4, 2, 3, 3, 64, 128), F32),
-        pltpu.VMEM((512, 256), BF16),
-        pltpu.VMEM((512, 256), BF16),
-        pltpu.VMEM((512, 512), BF16),
-        pltpu.VMEM((512, 512), BF16),
-        pltpu.VMEM((4, 128, 256), BF16),
-        pltpu.VMEM((4, 256, 256), BF16),
-        pltpu.VMEM((4, 256, 256), BF16),
-        pltpu.VMEM((4, 128, 128), F32),
+        pltpu.VMEM((5632, 256), BF16),
+        pltpu.VMEM((512, 128), F32),
         pltpu.VMEM((8, 128), F32),
         pltpu.VMEM((128, 1024), F32),
         pltpu.VMEM((8, 64, 128), F32),
@@ -644,7 +678,12 @@
         pltpu.VMEM((2, 3, 3, 8, 128), F32),
         pltpu.VMEM((4, 8, 8, 128), F32),
         pltpu.VMEM((4, 8, 8, 128), F32),
-        pltpu.SemaphoreType.DMA((9,)),
+        pltpu.VMEM((128, 1024), F32),
+        pltpu.VMEM((1024, 128), F32),
+        pltpu.VMEM((128, 1, 128), F32),
+        pltpu.VMEM((128, 1, 128), F32),
+        pltpu.SemaphoreType.DMA((2,)),
+        pltpu.SemaphoreType.DMA((3,)),
         pltpu.SemaphoreType.DMA((4,)),
         pltpu.SemaphoreType.DMA((4,)),
         pltpu.SemaphoreType.DMA((2 * ITERS,)),
@@ -659,7 +698,7 @@
         out_specs=anywhere,
         scratch_shapes=scratch,
         compiler_params=pltpu.CompilerParams(
-            collective_id=0, has_side_effects=True, vmem_limit_bytes=48 * 1024 * 1024
+            collective_id=0, has_side_effects=True, vmem_limit_bytes=50 * 1024 * 1024
         ),
     )(gauge_links, *operands)
 

time: 73.2 us -> 60.9 us (0.83)
  local copies, waits for them, and re-layouts: 10.4 us -> 1.41 us
  Pallas kernels: 62.2 us -> 59.3 us
    unnamed x19 -> x1, local copies, waits for them, and re-layouts: 10.4 us -> 1.41 us
    pallas_call x1, Pallas kernels: 62.2 us -> 59.3 us  [on_device(): pl.pallas_call(kernel, out_shape=jax.ShapeDtypeStruct(gauge_links.shape,...]
where the time goes in v2:
time: 60.9 us; the launch traced here: 60.8 us
  Pallas kernels  59.3 us (97%)
  local copies, waits for them, and re-layouts  1.41 us (2%)
    pallas_call x1, Pallas kernels, on_device(): pl.pallas_call(kernel, out_shape=jax.ShapeDtypeStruct(gauge_links.shape,...  59.3 us
    unnamed x1, local copies, waits for them, and re-layouts  1.41 us

profile of v2, /device:TPU:1, one launch (start us, length us, event | category | flops | bytes accessed | tf_op | source)
XLA Modules:
  0.0 60.8 jit_solution(8601658485825148076)
XLA Ops:
  0.0 59.3 %shard_map.37 = f32[4,2,3,3,1,8,1024]{6,5,4,3,2,1,0:T(8,128)S(1)} custom-call(f32[4,2,3,3,1,8,1024]{6,5,4,3,2,1,0:T(8,128)} %links_hbm.1, bf16[16384,256]{1,0:T(8,128)(2,1)} %constant.4.clone.tables_hbm, f32[16384,128]{1,0:T(8,128)} %constant.5.clone.waves_hbm), custom_call_target="tpu_custom_call" | custom-call | tf_op jit(solution)/shard_map/pallas_call | solution.py:694
  59.3 1.4 %copy.5 = f32[4,2,3,3,1,8,1024]{6,5,4,3,2,1,0:T(8,128)} copy(f32[4,2,3,3,1,8,1024]{6,5,4,3,2,1,0:T(8,128)S(1)} %shard_map.37) | data formatting | bytes 4718592

commit v3 on v2

--- a/solution.py
+++ b/solution.py
@@ -261,6 +261,7 @@
     ahead,
     link_out,
     link_in,
+    link_last,
     edge_out,
     edge_in,
     edge,
@@ -351,7 +352,6 @@
 
     def gather_fields(ct):
         row = row_of(ct)
-        wide = wide_row(ct)
         previous = pl.multiple_of(((ct + 7) % 8) * 8, 8)
         column = pl.multiple_of(ct * 128, 128)
         in_x = fields_of(tile_of(links, 0, row))
@@ -359,10 +359,15 @@
             total = before_x(in_x[f]) - in_x[f]
             here = along_y[f, pl.ds(row, 8), :]
             total += pltpu.roll(jnp.where(low_96, here, along_y[f, pl.ds(previous, 8), :]), 32, 1) - here
-            total += along_z[f, pl.ds(wide + 7, 8), :] - along_z[f, pl.ds(wide + 8, 8), :]
             delta[pl.ds(f * 8, 8), pl.ds(column, 128)] = total
         for f, value in enumerate(fields_of(tile_of(links, 3, row))):
             delta[pl.ds(64 + f * 8, 8), pl.ds(column, 128)] = value
+
+    def gather_depth(ct):
+        wide = wide_row(ct)
+        column = pl.ds(pl.multiple_of(ct * 128, 128), 128)
+        for f in range(8):
+            delta[pl.ds(f * 8, 8), column] += along_z[f, pl.ds(wide + 7, 8), :] - along_z[f, pl.ds(wide + 8, 8), :]
 
     def each_tile(body):
         def step(ct, carry):
@@ -518,7 +523,9 @@
 
     def make_gauge(ct):
         row = row_of(ct)
-        store_gauge(gauge, wide_row(ct), gauge_of([smooth[f, pl.ds(row, 8), :] for f in range(8)]))
+        here = gauge_of([smooth[f, pl.ds(row, 8), :] for f in range(8)])
+        store_gauge(gauge, wide_row(ct), here)
+        store_gauge(gauge, pl.multiple_of(ct * 16 + 8, 8), here)
         store_gauge(ahead, row, gauge_of([smooth[8 + f, pl.ds(row, 8), :] for f in range(8)]))
 
     def store_link(mu, row, rows):
@@ -579,6 +586,7 @@
     for f in range(8):
         along_z[f, pl.ds(7, 8, stride=16), :] = jnp.zeros((8, 128), F32)
     each_tile(gather_fields)
+    each_tile(gather_depth)
     each_tile(edge_fields)
     plane_forward(edge, edge_modes)
     pack_rows()
@@ -594,7 +602,7 @@
         last = iteration + 1 == ITERS
         slot = 4 * iteration
         if iteration > 0:
-            each_tile(gather_fields)
+            each_tile(gather_depth)
             plane_forward(delta, exchange.at[slot])
             exchange_start(slot)
         else:
@@ -624,13 +632,21 @@
                         out_hbm.at[mu, :, :, :, 0, :, pl.ds(ct * 128, 128)],
                         store_sem.at[mu],
                     ).start()
+        each_tile(rotate_z)
+        if not last:
+            each_tile(spread_fields)
+            each_tile(gather_fields)
         to_before.wait_recv()
         halo = gauge_of([edge_in[high_way, f] for f in range(8)])
+        left = load_gauge(gauge, pl.ds(7, 8, stride=16))
+        before_last = link_out if iteration == 0 else link_last
+        top = rotated_link(left, lambda part, i, k: before_last[part, i, k], halo)
         for part in range(2):
             for i in range(3):
                 for k in range(3):
-                    gauge[part, i, k, pl.ds(8, 8, stride=16), :] = halo[i][k][part]
-        each_tile(rotate_z)
+                    links[2, part, i, k, pl.ds(7, 8, stride=8), :] = top[i][k][part]
+                    if not last:
+                        link_last[part, i, k] = top[i][k][part]
         if last:
             for ct in range(8):
                 pltpu.make_async_copy(
@@ -639,12 +655,13 @@
                     store_sem.at[2],
                 ).start()
         else:
+            for f, value in enumerate(fields_of(lambda part, i, k: top[i][k][part])):
+                along_z[f, pl.ds(15, 8, stride=16), :] = value
             to_after.wait_recv()
             link_copy.wait_recv()
             left = gauge_of([edge_in[low_way, f] for f in range(8)])
             right = load_gauge(gauge, pl.ds(0, 8, stride=16))
             below = rotated_link(left, lambda part, i, k: link_in[part, i, k], right)
-            each_tile(spread_fields)
             for f, value in enumerate(fields_of(lambda part, i, k: below[i][k][part])):
                 along_z[f, pl.ds(7, 8, stride=16), :] = value
             to_after.wait_send()
@@ -674,6 +691,7 @@
         pltpu.VMEM((16, 64, 128), F32),
         pltpu.VMEM((2, 3, 3, 128, 128), F32),
         pltpu.VMEM((2, 3, 3, 64, 128), F32),
+        pltpu.VMEM((2, 3, 3, 8, 128), F32),
         pltpu.VMEM((2, 3, 3, 8, 128), F32),
         pltpu.VMEM((2, 3, 3, 8, 128), F32),
         pltpu.VMEM((4, 8, 8, 128), F32),

time: 60.9 us -> 60.5 us (level)
  no operation moved by 1% of the time
where the time goes in v3:
time: 60.5 us; the launch traced here: 60.4 us
  Pallas kernels  59 us (98%)
  local copies, waits for them, and re-layouts  1.41 us (2%)
    pallas_call x1, Pallas kernels, on_device(): pl.pallas_call(kernel, out_shape=jax.ShapeDtypeStruct(gauge_links.shape,...  59 us
    unnamed x1, local copies, waits for them, and re-layouts  1.41 us

profile of v3, /device:TPU:1, one launch (start us, length us, event | category | flops | bytes accessed | tf_op | source)
XLA Modules:
  0.0 60.4 jit_solution(14105901859469801686)
XLA Ops:
  0.0 59.0 %shard_map.37 = f32[4,2,3,3,1,8,1024]{6,5,4,3,2,1,0:T(8,128)S(1)} custom-call(f32[4,2,3,3,1,8,1024]{6,5,4,3,2,1,0:T(8,128)} %links_hbm.1, bf16[16384,256]{1,0:T(8,128)(2,1)} %constant.4.clone.tables_hbm, f32[16384,128]{1,0:T(8,128)} %constant.5.clone.waves_hbm), custom_call_target="tpu_custom_call" | custom-call | tf_op jit(solution)/shard_map/pallas_call | solution.py:712
  59.0 1.4 %copy.5 = f32[4,2,3,3,1,8,1024]{6,5,4,3,2,1,0:T(8,128)} copy(f32[4,2,3,3,1,8,1024]{6,5,4,3,2,1,0:T(8,128)S(1)} %shard_map.37) | data formatting | bytes 4718592
